TPU v7x, 1024 devices: a whole 4x8x16 slice. The times are simulated.
1024 devices in a mesh: dp: 16 (over z), expert: 64 (over x, y, core).
Axes of the slice: x: 4, y: 8, z: 16, core: 2. Of those that a mesh axis runs over, the one named last changes fastest.
Arguments:
- tokens: bfloat16 [1024, 3584], P(('dp', 'expert')), may hold values from -6 to 6
- expert_ids: int32 [1024, 8], P('dp'), may hold values from 0 to 63, as said below
- gates: bfloat16 [1024, 8], P('dp'), may hold values from 0.099609375 to 1
- w_gate: bfloat16 [64, 3584, 2048], P('expert', None, 'dp'), may hold values from -0.09375 to 0.09375
- w_up: bfloat16 [64, 3584, 2048], P('expert', None, 'dp'), may hold values from -0.09375 to 0.09375
- w_down: bfloat16 [64, 2048, 3584], P('expert', 'dp'), may hold values from -0.125 to 0.125
- cotangent: bfloat16 [1024, 3584], P(('dp', 'expert')), may hold values from -6 to 6
Outputs:
- mixed: bfloat16 [1024, 3584], P(('dp', 'expert'))
- grad_tokens: bfloat16 [1024, 3584], P(('dp', 'expert'))
- grad_gates: float32 [1024, 8], P(('dp', 'expert'))
Inputs may be any that keep to these rules, and one draw needn't show every extreme that they name: `expert_ids`: each row names 8 distinct experts, exactly two from each of four of the 8 groups of 8 consecutive experts. In each aligned block of 64 rows no expert is named by more than 9 rows, and some expert by exactly 9.
All inputs are finite; a program needn't handle non-finite values.
Results may differ from a plain program's by a relative error of at most 0.035.
Values may be sent and summed in bfloat16 or wider, within the bound.
No kernel may reach another device: no remote copies, remote signals or barrier semaphores. Data moves between devices by JAX's collectives and lax.ppermute only.
A program may use at most 32 MiB of HBM per device.

v0:
```python
import jax
import jax.numpy as jnp
from jax import lax
from jax.sharding import PartitionSpec as P


def spread_row(values):
    return lax.all_gather(values, "expert", axis=0, tiled=True)


def spread_dp(expert_rows, row_fn):
    return row_fn(lax.all_gather(expert_rows, "dp", axis=1, tiled=True), jnp.int32(0))


def sum_hidden(term_fn, slot_count):
    return lax.psum_scatter(
        term_fn(jnp.int32(0), lax.axis_size("dp") * slot_count).astype(jnp.bfloat16),
        "dp",
        scatter_dimension=0,
        tiled=True,
    ).astype(jnp.float32)


def local(tokens, expert_ids, gates, w_gate, w_up, w_down, cotangent):
    device_count = lax.axis_size("expert")
    held_experts = w_gate.shape[0]
    hidden = w_gate.shape[2]
    own_tokens = tokens.shape[0]
    shard_tokens = own_tokens * device_count
    experts_all = held_experts * device_count
    group_size = experts_all // 8
    capacity = shard_tokens // group_size + 1
    position = lax.axis_index("expert")
    owned_ids = position * held_experts + jnp.arange(held_experts, dtype=jnp.int32)
    matches = (expert_ids[:, :, None] == owned_ids).astype(jnp.int32)
    member = jnp.sum(matches, axis=1)
    slot_index = jnp.cumsum(member, axis=0) - 1
    slot_range = jnp.arange(capacity, dtype=jnp.int32)
    chooser = ((member[:, :, None] > 0) & (slot_index[:, :, None] == slot_range)).astype(
        jnp.bfloat16
    )
    gate_sel = jnp.einsum("tkj,tk->tj", matches.astype(jnp.float32), gates.astype(jnp.float32))
    gathered = spread_row(tokens)
    expert_input = jnp.einsum(
        "tjc,td->jcd", chooser, gathered, preferred_element_type=jnp.float32
    ).astype(jnp.bfloat16)

    def project_in(piece, start):
        gate_part = jnp.einsum("jnd,jdh->jnh", piece, w_gate, preferred_element_type=jnp.float32)
        up_part = jnp.einsum("jnd,jdh->jnh", piece, w_up, preferred_element_type=jnp.float32)
        return jnp.concatenate([gate_part, up_part], axis=2)

    pre_acts = spread_dp(expert_input, project_in)
    gate_pre = pre_acts[..., :hidden]
    up_pre = pre_acts[..., hidden:]
    activated = (gate_pre * jax.nn.sigmoid(gate_pre) * up_pre).astype(jnp.bfloat16)

    def project_out(start, count):
        return jnp.einsum("jnh,jhd->njd", activated, w_down, preferred_element_type=jnp.float32)

    out_rows = sum_hidden(project_out, capacity).astype(jnp.bfloat16)
    cot_all = spread_row(cotangent)
    cot_rows = jnp.einsum("tjc,td->jcd", chooser, cot_all, preferred_element_type=jnp.float32)
    gate_rows = jnp.einsum("tjc,tj->jc", chooser.astype(jnp.float32), gate_sel)
    grad_rows = (cot_rows * gate_rows[..., None]).astype(jnp.bfloat16)

    def grad_in(piece, start):
        grad_hid = jnp.einsum("jnd,jhd->jnh", piece, w_down, preferred_element_type=jnp.float32)
        gate_here = pre_acts[..., :hidden]
        up_here = pre_acts[..., hidden:]
        sig_gate = jax.nn.sigmoid(gate_here)
        grad_gate = grad_hid * up_here * sig_gate * (1.0 + gate_here * (1.0 - sig_gate))
        grad_up = grad_hid * gate_here * sig_gate
        return jnp.concatenate([grad_gate, grad_up], axis=2).astype(jnp.bfloat16)

    grad_acts = spread_dp(grad_rows, grad_in)

    def grad_out(start, count):
        back = jnp.einsum(
            "jnh,jdh->njd", grad_acts[..., :hidden], w_gate, preferred_element_type=jnp.float32
        )
        return back + jnp.einsum(
            "jnh,jdh->njd", grad_acts[..., hidden:], w_up, preferred_element_type=jnp.float32
        )

    dx_rows = sum_hidden(grad_out, capacity).astype(jnp.bfloat16)
    dense_out = jnp.einsum(
        "tjc,cjd->jtd", chooser, out_rows, preferred_element_type=jnp.float32
    ).astype(jnp.bfloat16)
    received = lax.all_to_all(dense_out, "expert", split_axis=1, concat_axis=0, tiled=True)
    own_ids = lax.dynamic_slice_in_dim(expert_ids, position * own_tokens, own_tokens, 0)
    own_gates = lax.dynamic_slice_in_dim(gates, position * own_tokens, own_tokens, 0).astype(
        jnp.float32
    )
    route_onehot = (own_ids[:, :, None] == jnp.arange(experts_all, dtype=jnp.int32)).astype(
        jnp.float32
    )
    per_route = jnp.einsum("tkx,xtd->tkd", route_onehot, received.astype(jnp.float32))
    mixed = jnp.einsum("tk,tkd->td", own_gates, per_route).astype(jnp.bfloat16)
    grad_gates = jnp.einsum("tkd,td->tk", per_route, cotangent.astype(jnp.float32))
    dense_dx = jnp.einsum(
        "tjc,cjd->jtd", chooser, dx_rows, preferred_element_type=jnp.float32
    ).astype(jnp.bfloat16)
    received_dx = lax.all_to_all(dense_dx, "expert", split_axis=1, concat_axis=0, tiled=True)
    grad_tokens = jnp.einsum("tkx,xtd->td", route_onehot, received_dx.astype(jnp.float32)).astype(
        jnp.bfloat16
    )
    return (mixed, grad_tokens, grad_gates)


def solution(mesh):
    return jax.shard_map(
        local,
        mesh=mesh,
        in_specs=(
            P(("dp", "expert"), None),
            P("dp", None),
            P("dp", None),
            P("expert", None, "dp"),
            P("expert", None, "dp"),
            P("expert", "dp", None),
            P(("dp", "expert"), None),
        ),
        out_specs=(P(("dp", "expert"), None), P(("dp", "expert"), None), P(("dp", "expert"), None)),
        check_vma=False,
    )
```

profile of v0, /device:TPU:1, one launch (start us, length us, event | category | flops | bytes accessed | tf_op | source)
XLA Modules:
  0.0 420.6 jit_solution(2557860394436813345)
XLA Ops:
  7.2 0.8 fusion.47
  8.4 61.9 %all-gather.4 = bf16[64,1,3584]{2,1,0:T(2,128)(2,1)S(1)} all-gather(bf16[1,1,3584]{2,1,0:T(2,128)(2,1)} %bitcast.101), channel_id=1, replica_groups=mesh['dp'=16,'expert'=64] {'expert'}, dimensions={0}, use_global_device_ids=true | all-gather | bytes 465920 | tf_op jit(solution)/shard_map/all_gather | solution.py:8
  70.7 39.2 %all-gather.5 = bf16[16,9,3584]{2,1,0:T(8,128)(2,1)S(1)} all-gather(bf16[1,9,3584]{2,1,0:T(8,128)(2,1)S(1)} %fusion.7), channel_id=3, replica_groups=mesh['dp'=16,'expert'=64] {'dp'}, dimensions={0}, use_global_device_ids=true | all-gather | bytes 1096704 | tf_op jit(solution)/shard_map/all_gather | solution.py:12
  109.9 1.3 reshape.413
  111.2 55.5 %all-gather.2 = bf16[64,1,3584]{2,1,0:T(2,128)(2,1)S(1)} all-gather(bf16[1,1,3584]{2,1,0:T(2,128)(2,1)S(1)} %bitcast.100), channel_id=1, replica_groups=mesh['dp'=16,'expert'=64] {'expert'}, dimensions={0}, use_global_device_ids=true | all-gather | bytes 465920 | tf_op jit(solution)/shard_map/all_gather | solution.py:8
  167.0 35.5 %all-gather.3 = bf16[16,9,3584]{2,1,0:T(8,128)(2,1)} all-gather(bf16[1,9,3584]{2,1,0:T(8,128)(2,1)S(1)} %fusion.6), channel_id=2, replica_groups=mesh['dp'=16,'expert'=64] {'dp'}, dimensions={0}, use_global_device_ids=true | all-gather | bytes 1096704 | tf_op jit(solution)/shard_map/all_gather | solution.py:12
  202.5 1.7 reshape.409
  204.7 0.7 copy-done.3
  206.3 1.4 fusion.1
  208.2 1.4 fusion.2
  209.6 1.3 dynamic-slice
  211.5 136.6 %all-reduce.5.cloned.1.call-done = (bf16[144,1,3584]{2,0,1:T(8,128)(2,1)}, bf16[144,1,3584]{2,0,1:T(8,128)(2,1)}) async-done(((bf16[144,1,3584]{2,0,1:T(8,128)(2,1)}, bf16[144,1,3584]{2,0,1:T(8,128)(2,1)}), (bf16[144,1,3584]{2,0,1:T(8,128)(2,1)}, bf16[144,1,3584]{2,0,1:T(8,128)(2,1)})) %all-reduce.5.cloned.1.call-update) | async-done | bytes 2064400
  348.1 1.2 fusion.4
  349.4 0.7 copy.51
  350.6 3.5 reduce.16
  354.1 0.9 reshape.440
  355.0 18.5 %all-to-all-start.1 = ((bf16[64,2,1792]{2,1,0:T(2,128)(2,1)}), bf16[64,2,1792]{2,1,0:T(2,128)(2,1)S(1)}, u32[]{:S(2)}, u32[]{:S(2)}) async-start(bf16[64,2,1792]{2,1,0:T(2,128)(2,1)} %reshape.440), calls=%async_computation.1 | async-start | bytes 917504 | tf_op jit(solution)/shard_map/all_to_all | solution.py:104
  373.5 1.3 fusion.3
  374.8 0.7 copy.52
  375.6 3.5 reduce.15
  379.1 0.9 reshape.438
  379.9 9.5 %all-to-all-done.1 = bf16[64,2,1792]{2,1,0:T(2,128)(2,1)S(1)} async-done(((bf16[64,2,1792]{2,1,0:T(2,128)(2,1)}), bf16[64,2,1792]{2,1,0:T(2,128)(2,1)S(1)}, u32[]{:S(2)}, u32[]{:S(2)}) %all-to-all-start.1) | async-done | bytes 458784 | tf_op jit(solution)/shard_map/all_to_all | solution.py:104
  389.5 6.3 %all-to-all-start = ((bf16[64,2,1792]{2,1,0:T(2,128)(2,1)}), bf16[64,2,1792]{2,1,0:T(2,128)(2,1)S(1)}, u32[]{:S(2)}, u32[]{:S(2)}) async-start(bf16[64,2,1792]{2,1,0:T(2,128)(2,1)} %reshape.438), calls=%async_computation | async-start | bytes 917504 | tf_op jit(solution)/shard_map/all_to_all | solution.py:90
  397.4 14.3 %all-to-all-done = bf16[64,2,1792]{2,1,0:T(2,128)(2,1)S(1)} async-done(((bf16[64,2,1792]{2,1,0:T(2,128)(2,1)}), bf16[64,2,1792]{2,1,0:T(2,128)(2,1)S(1)}, u32[]{:S(2)}, u32[]{:S(2)}) %all-to-all-start) | async-done | bytes 458784 | tf_op jit(solution)/shard_map/all_to_all | solution.py:90
  (41 shorter events, 7.1 us)
Async XLA Ops:
  7.2 198.7 %copy-start = (bf16[1,128,3584]{2,1,0:T(8,128)(2,1)S(1)}, bf16[1,128,3584]{2,1,0:T(8,128)(2,1)}, u32[]{:S(2)}) copy-start(bf16[1,128,3584]{2,1,0:T(8,128)(2,1)} %param.12) | copy-start | bytes 2752516
  7.2 341.0 %all-reduce.5.cloned.1.call-start = ((), (), s32[]{:S(2)}) async-start(), calls=%async_computation.2 | async-start | bytes 4128768
  70.7 40.5 %copy-start.5 = (bf16[1,3584]{1,0:T(2,128)(2,1)S(1)}, bf16[1,3584]{1,0:T(2,128)(2,1)}, u32[]{:S(2)}) copy-start(bf16[1,3584]{1,0:T(2,128)(2,1)} %param.7) | copy-start | bytes 21508
  167.0 37.2 %copy-start.2 = (bf16[1,3584,128]{2,1,0:T(8,128)(2,1)S(1)}, bf16[1,3584,128]{2,1,0:T(8,128)(2,1)}, u32[]{:S(2)}) copy-start(bf16[1,3584,128]{2,1,0:T(8,128)(2,1)} %param.10) | copy-start | bytes 2752516
  204.2 1.2 copy-start.3
  204.3 1.6 copy-start.1
  355.0 34.4 %all-to-all-start.1 = ((bf16[64,2,1792]{2,1,0:T(2,128)(2,1)}), bf16[64,2,1792]{2,1,0:T(2,128)(2,1)S(1)}, u32[]{:S(2)}, u32[]{:S(2)}) async-start(bf16[64,2,1792]{2,1,0:T(2,128)(2,1)} %reshape.440), calls=%async_computation.1 | async-start | bytes 917504 | tf_op jit(solution)/shard_map/all_to_all | solution.py:104
  374.8 21.0 %copy-start.4 = (s32[64,8]{0,1:T(8,128)S(1)}, s32[64,8]{0,1:T(8,128)}, u32[]{:S(2)}) copy-start(s32[64,8]{0,1:T(8,128)} %param.8) | copy-start | bytes 6148
  374.8 21.1 %copy-start.7 = (bf16[64,8]{0,1:T(8,128)(2,1)S(1)}, bf16[64,8]{0,1:T(8,128)(2,1)}, u32[]{:S(2)}) copy-start(bf16[64,8]{0,1:T(8,128)(2,1)} %param.9) | copy-start | bytes 3076
  389.5 22.2 %all-to-all-start = ((bf16[64,2,1792]{2,1,0:T(2,128)(2,1)}), bf16[64,2,1792]{2,1,0:T(2,128)(2,1)S(1)}, u32[]{:S(2)}, u32[]{:S(2)}) async-start(bf16[64,2,1792]{2,1,0:T(2,128)(2,1)} %reshape.438), calls=%async_computation | async-start | bytes 917504 | tf_op jit(solution)/shard_map/all_to_all | solution.py:90
  395.8 16.5 %copy-start.6 = (bf16[1,3584]{1,0:T(2,128)(2,1)S(1)}, bf16[1,3584]{1,0:T(2,128)(2,1)}, u32[]{:S(2)}) copy-start(bf16[1,3584]{1,0:T(2,128)(2,1)} %param.13) | copy-start | bytes 21508
Sparse Core Ops, SparseCore 0:
  209.7 138.3 all-reduce.4
where the time goes:
time: 421 us
  blocking collectives  192 us (46%)
  waiting for transfers between devices  160 us (38%)
  starting transfers between devices  24.8 us (6%)
  between operations  14.9 us (4%)
  local copies, waits for them, and re-layouts  11.1 us (3%)
  matrix products  9.1 us (2%)
  other arithmetic  8.14 us (2%)
    unnamed x2, waiting for transfers between devices  137 us
    all_gather x2, blocking collectives, spread_row(): return lax.all_gather(values, 'expert', axis=0, tiled=True)  117 us
    all_gather x2, blocking collectives, spread_dp(): lax.all_gather(expert_rows, 'dp', axis=1, tiled=True)  74.7 us
    all_to_all x1, starting transfers between devices, local(): lax.all_to_all(dense_dx, 'expert', split_axis=1, concat_axis=0, tiled=True)  18.5 us
    all_to_all x1, waiting for transfers between devices, local(): lax.all_to_all(dense_out, 'expert', split_axis=1, concat_axis=0, tiled=True)  14.3 us
    all_to_all x1, waiting for transfers between devices, local(): lax.all_to_all(dense_dx, 'expert', split_axis=1, concat_axis=0, tiled=True)  9.51 us
  transfers between devices with their start and end apart: 3, of which 3 were waited for; matrix products, arithmetic and copies ran while one was open for 2% of the time, Pallas kernels for 0%

commit v1 on v0

v1 whole, which is shorter than its diff:
```python
import jax
import jax.numpy as jnp
import numpy as np
from jax import lax
from jax.sharding import Mesh, PartitionSpec as P

F32 = jnp.float32
BF16 = jnp.bfloat16
CAP = 9
QN = 4
PIECES = 2 * QN
PACK = PIECES * CAP
ZA, ZC = 4, 4
EXTRA = 128
ZAXES = ("za", "zc")
PLANE = ("x", "y")


def shift_z(values, step):
    n = ZA * ZC
    return lax.ppermute(values, ZAXES, [(i, (i + step) % n) for i in range(n)])


def swap_core(values):
    return lax.ppermute(values, "c", [(0, 1), (1, 0)])


def unpack_matrix():
    rows = np.arange(ZA * PACK)
    slot = rows % CAP
    chunk = rows // CAP % ZA
    half = rows // (CAP * ZA) % 2
    piece = rows // (CAP * ZA * 2)
    source = ((chunk * 2 + half) * QN + piece) * CAP + slot
    matrix = np.zeros((ZA * PACK, ZA * PACK), np.float32)
    matrix[rows, source] = 1
    return matrix


def dot(a, b, dims=((1,), (0,))):
    return lax.dot_general(a, b, (dims, ((), ())), preferred_element_type=F32)


def local(tokens, expert_ids, gates, w_gate, w_up, w_down, cotangent):
    width = tokens.shape[1]
    lanes = width // QN
    half_width = width // 2
    chips = lax.axis_size(PLANE)
    block = expert_ids.shape[0]
    topk = expert_ids.shape[1]
    core = lax.axis_index("c").astype(jnp.int32)
    expert = lax.axis_index(PLANE).astype(jnp.int32) * 2 + core
    sibling = expert + 1 - 2 * core
    w_gate, w_up, w_down = w_gate[0], w_up[0], w_down[0]

    payload = jnp.concatenate(
        [tokens.reshape(QN, lanes), cotangent.reshape(QN, lanes)], axis=0
    )
    spread = jnp.broadcast_to(payload[None], (chips, PIECES, lanes))
    gathered = lax.all_to_all(spread, PLANE, 0, 0, tiled=True).reshape(chips * PIECES, lanes)

    ids = expert_ids.T
    named = ids == expert
    member = jnp.stack([jnp.any(named, axis=0), jnp.any(ids == sibling, axis=0)])
    token_row = lax.broadcasted_iota(jnp.int32, (block, block), 0)
    token_col = lax.broadcasted_iota(jnp.int32, (block, block), 1)
    earlier = (token_row < token_col).astype(BF16)
    before = dot(member.astype(BF16), earlier)
    place = jnp.where(member, before + 1.0, 0.0)
    spot = lax.broadcasted_iota(jnp.int32, (block, chips * PIECES), 1)
    token_at = lax.broadcasted_iota(jnp.int32, (block, chips * PIECES), 0)
    expand = (token_at == 2 * (spot // PIECES) + core).astype(BF16)
    place_cols = dot(place.astype(BF16), expand)
    row = lax.broadcasted_iota(jnp.int32, (2 * PACK, chips * PIECES), 0)
    col = lax.broadcasted_iota(jnp.int32, (2 * PACK, chips * PIECES), 1)
    held = jnp.where(row < PACK, place_cols[0:1], place_cols[1:2])
    choose = (
        (held == (row % CAP + 1).astype(F32)) & (row // CAP % PIECES == col % PIECES)
    ).astype(BF16)

    gate_of = jnp.sum(jnp.where(named, gates.T.astype(F32), 0.0), axis=0)
    slot_row = lax.broadcasted_iota(jnp.int32, (PACK, block), 0) % CAP + 1
    in_slot = place[0:1] == slot_row.astype(F32)
    gate_rows = jnp.sum(jnp.where(in_slot, gate_of[None], 0.0), axis=1, keepdims=True)
    route_rows = dot(in_slot[:CAP].astype(BF16), named.astype(BF16), ((1,), (1,)))

    chosen = dot(choose, gathered).astype(BF16)
    packed = chosen[:PACK] + swap_core(chosen[PACK:])

    turn = jnp.asarray(unpack_matrix(), BF16)
    strided = lax.all_gather(packed, "za", axis=0).reshape(ZA * PACK, lanes)
    turned = dot(turn, strided).astype(BF16)
    group = turned.shape[0] // QN
    here = jnp.concatenate([turned[q * group : (q + 1) * group] for q in range(QN)], axis=1)
    below = shift_z(here, 1)
    above = shift_z(here, -1)
    far_left = shift_z(below[:, :half_width], 1)
    far_right = shift_z(above[:, half_width:], -1)
    far = jnp.concatenate([far_left, far_right], axis=1)
    rows = group // 2

    def expert_terms(values):
        gate_pre = dot(values, w_gate)[:rows]
        up_pre = dot(values, w_up)[:rows]
        grad_hid = dot(values, w_down, ((1,), (1,)))[rows:]
        sig = jax.nn.sigmoid(gate_pre)
        hid = (gate_pre * sig * up_pre).astype(BF16)
        grad_gate = (grad_hid * up_pre * sig * (1.0 + gate_pre * (1.0 - sig))).astype(BF16)
        grad_up = (grad_hid * gate_pre * sig).astype(BF16)
        none = jnp.zeros_like(hid)
        out = dot(jnp.concatenate([hid, none], axis=0), w_down)
        out = out + dot(jnp.concatenate([none, grad_gate], axis=0), w_gate, ((1,), (1,)))
        out = out + dot(jnp.concatenate([none, grad_up], axis=0), w_up, ((1,), (1,)))
        return out.astype(BF16)

    terms_far = expert_terms(far)
    terms_here, terms_below, terms_above = (
        expert_terms(here),
        expert_terms(below),
        expert_terms(above),
    )

    back_left = shift_z(terms_far[:, :half_width], -1)
    back_right = shift_z(terms_far[:, half_width:], 1)
    low = jnp.concatenate(
        [
            (terms_below[:, :half_width].astype(F32) + back_left.astype(F32)).astype(BF16),
            terms_below[:, half_width:],
        ],
        axis=1,
    )
    high = jnp.concatenate(
        [
            terms_above[:, :half_width],
            (terms_above[:, half_width:].astype(F32) + back_right.astype(F32)).astype(BF16),
        ],
        axis=1,
    )
    from_above = shift_z(low, -1)
    from_below = shift_z(high, 1)
    summed = (
        terms_here.astype(F32) + from_above.astype(F32) + from_below.astype(F32)
    ).astype(BF16)
    stacked = jnp.concatenate(
        [summed[:, q * lanes : (q + 1) * lanes] for q in range(QN)], axis=0
    )
    outgoing = dot(turn, stacked, ((0,), (0,))).astype(BF16).reshape(ZA, PACK, lanes)
    arrived = lax.all_to_all(outgoing, "za", 0, 0, tiled=True)
    results = jnp.sum(arrived.astype(F32), axis=0)

    half = PACK // 2
    value_rows = results[:half].astype(BF16).astype(F32)
    dots = jnp.sum(value_rows * packed[half:].astype(F32), axis=1)
    slot_dots = jnp.sum(dots.reshape(QN, CAP), axis=0)[:, None]
    dots_high = lax.reduce_precision(slot_dots, 8, 7)
    dots_low = slot_dots - dots_high
    carried = jnp.concatenate([dots_high * route_rows, dots_low * route_rows], axis=1)
    carried = jnp.pad(carried, ((0, PACK - CAP), (0, EXTRA - 2 * topk)))
    scaled = jnp.concatenate([results * gate_rows, carried], axis=1).astype(BF16)
    both = jnp.concatenate([scaled, swap_core(scaled)], axis=0)

    dense = dot(choose, both, ((0,), (0,))).astype(BF16)
    dense = dense.reshape(chips, PIECES, lanes + EXTRA)
    mine = lax.all_to_all(dense, PLANE, 0, 0, tiled=True)
    total = jnp.sum(mine.astype(F32), axis=0)
    mixed = total[:QN, :lanes].astype(BF16).reshape(1, width)
    grad_tokens = total[QN:, :lanes].astype(BF16).reshape(1, width)
    grad_gates = total[0:1, lanes : lanes + topk] + total[0:1, lanes + topk : lanes + 2 * topk]
    return mixed, grad_tokens, grad_gates


def solution(mesh, plane=(4, 8, 2)):
    fine = Mesh(mesh.devices.reshape((ZA, ZC) + plane), ZAXES + PLANE + ("c",))
    rows = P(ZAXES + PLANE + ("c",), None)
    experts = PLANE + ("c",)
    return jax.shard_map(
        local,
        mesh=fine,
        in_specs=(
            rows,
            P(ZAXES, None),
            P(ZAXES, None),
            P(experts, None, ZAXES),
            P(experts, None, ZAXES),
            P(experts, ZAXES, None),
            rows,
        ),
        out_specs=(rows, rows, rows),
        check_vma=False,
    )
```

time: 421 us -> 198 us (0.47)
  the two profiles are of different devices: /device:TPU:1 before, /device:TPU:200 now
where the time goes in v1:
time: 198 us; the launch traced here: 197 us
  waiting for transfers between devices  67.1 us (34%)
  blocking collectives  62.1 us (31%)
  starting transfers between devices  44.3 us (22%)
  matrix products  14.5 us (7%)
  local copies, waits for them, and re-layouts  5.33 us (3%)
  other arithmetic  2.43 us (1%)
    all_gather x1, blocking collectives, local(): strided = lax.all_gather(packed, 'za', axis=0).reshape(ZA * PACK, lanes)  38 us
    ppermute x8, waiting for transfers between devices, shift_z(): return lax.ppermute(values, ZAXES, [(i, (i + step) % n) for i in range(n)])  25 us
    all_to_all x1, waiting for transfers between devices, local(): arrived = lax.all_to_all(outgoing, 'za', 0, 0, tiled=True)  25 us
    all_to_all x1, blocking collectives, local(): mine = lax.all_to_all(dense, PLANE, 0, 0, tiled=True)  24.1 us
    ppermute x8, starting transfers between devices, shift_z(): return lax.ppermute(values, ZAXES, [(i, (i + step) % n) for i in range(n)])  23.6 us
    dot_general x34, matrix products, dot(): return lax.dot_general(a, b, (dims, ((), ())), preferred_element_type=F32)  14.5 us
    all_to_all x1, waiting for transfers between devices, local(): lax.all_to_all(spread, PLANE, 0, 0, tiled=True)  14.4 us
    all_to_all x1, starting transfers between devices, local(): lax.all_to_all(spread, PLANE, 0, 0, tiled=True)  10.2 us
  transfers between devices with their start and end apart: 12, of which 10 were waited for; matrix products, arithmetic and copies ran while one was open for 4% of the time, Pallas kernels for 0%

profile of v1, /device:TPU:200, one launch (start us, length us, event | category | flops | bytes accessed | tf_op | source)
XLA Modules:
  0.0 196.9 jit_solution(3943954566514387006)
XLA Ops:
  2.4 10.2 %all-to-all-start = ((bf16[32,8,896]{2,1,0:T(8,128)(2,1)}), bf16[32,8,896]{2,1,0:T(8,128)(2,1)S(1)}, u32[]{:S(2)}, u32[]{:S(2)}) async-start(bf16[32,8,896]{2,1,0:T(8,128)(2,1)} %broadcast_in_dim.54), calls=%async_computation | async-start | bytes 917504 | tf_op jit(solution)/shard_map/all_to_all | solution.py:60
  14.4 14.4 %all-to-all-done = bf16[32,8,896]{2,1,0:T(8,128)(2,1)S(1)} async-done(((bf16[32,8,896]{2,1,0:T(8,128)(2,1)}), bf16[32,8,896]{2,1,0:T(8,128)(2,1)S(1)}, u32[]{:S(2)}, u32[]{:S(2)}) %all-to-all-start) | async-done | bytes 458784 | tf_op jit(solution)/shard_map/all_to_all | solution.py:60
  29.2 1.9 collective-permute-start
  31.1 1.3 collective-permute-done
  32.5 38.0 %all-gather = bf16[288,896]{1,0:T(8,128)(2,1)S(1)} all-gather(bf16[72,896]{1,0:T(8,128)(2,1)S(1)} %slice_add_fusion), channel_id=2, replica_groups=mesh['za'=4,'zc'=4,'x'=4,'y'=8,'c'=2] {'za'}, dimensions={0}, use_global_device_ids=true | all-gather | bytes 645120 | tf_op jit(solution)/shard_map/all_gather | solution.py:91
  71.0 2.1 %collective-permute-start.1 = (bf16[72,3584]{1,0:T(8,128)(2,1)S(1)}, bf16[72,3584]{1,0:T(8,128)(2,1)S(1)}, u32[]{:S(2)}, u32[]{:S(2)}) collective-permute-start(bf16[72,3584]{1,0:T(8,128)(2,1)S(1)} %pad_maximum_fusion), channel_id=1, source_target_pairs={{0,64},{64,128},{128,192},{192,256},{256,320},{320,384},{384,448},... | collective-permute-start | bytes 1548296 | tf_op jit(solution)/shard_map/ppermute | solution.py:21
  73.1 3.9 %collective-permute-start.3 = (bf16[72,3584]{1,0:T(8,128)(2,1)S(1)}, bf16[72,3584]{1,0:T(8,128)(2,1)S(1)}, u32[]{:S(2)}, u32[]{:S(2)}) collective-permute-start(bf16[72,3584]{1,0:T(8,128)(2,1)S(1)} %pad_maximum_fusion), channel_id=1, source_target_pairs={{0,960},{64,0},{128,64},{192,128},{256,192},{320,256},{384,320},{4... | collective-permute-start | bytes 1548296 | tf_op jit(solution)/shard_map/ppermute | solution.py:21
  78.1 8.8 %collective-permute-done.1 = bf16[72,3584]{1,0:T(8,128)(2,1)S(1)} collective-permute-done((bf16[72,3584]{1,0:T(8,128)(2,1)S(1)}, bf16[72,3584]{1,0:T(8,128)(2,1)S(1)}, u32[]{:S(2)}, u32[]{:S(2)}) %collective-permute-start.1) | collective-permute-done | bytes 516128 | tf_op jit(solution)/shard_map/ppermute | solution.py:21
  86.9 3.4 %collective-permute-start.2 = (bf16[72,1792]{1,0:T(8,128)(2,1)S(1)}, bf16[72,1792]{1,0:T(8,128)(2,1)S(1)}, u32[]{:S(2)}, u32[]{:S(2)}) collective-permute-start(bf16[72,1792]{1,0:T(8,128)(2,1)S(1)} %slice.192), channel_id=1, source_target_pairs={{0,64},{64,128},{128,192},{192,256},{256,320},{320,384},{384,448},... | collective-permute-start | bytes 774152 | tf_op jit(solution)/shard_map/ppermute | solution.py:21
  90.3 2.4 %collective-permute-start.4 = (bf16[72,1792]{1,0:T(8,128)(2,1)S(1)}, bf16[72,1792]{1,0:T(8,128)(2,1)S(1)}, u32[]{:S(2)}, u32[]{:S(2)}) collective-permute-start(bf16[72,1792]{1,0:T(8,128)(2,1)S(1)} %slice.193), channel_id=1, source_target_pairs={{0,960},{64,0},{128,64},{192,128},{256,192},{320,256},{384,320},{4... | collective-permute-start | bytes 774152 | tf_op jit(solution)/shard_map/ppermute | solution.py:21
  97.5 3.4 %collective-permute-done.4 = bf16[72,1792]{1,0:T(8,128)(2,1)S(1)} collective-permute-done((bf16[72,1792]{1,0:T(8,128)(2,1)S(1)}, bf16[72,1792]{1,0:T(8,128)(2,1)S(1)}, u32[]{:S(2)}, u32[]{:S(2)}) %collective-permute-start.4) | collective-permute-done | bytes 258080 | tf_op jit(solution)/shard_map/ppermute | solution.py:21
  103.6 1.9 collective-permute-start.7
  106.2 3.9 %collective-permute-start.5 = (bf16[72,1792]{1,0:T(8,128)(2,1)S(1)}, bf16[72,1792]{1,0:T(8,128)(2,1)S(1)}, u32[]{:S(2)}, u32[]{:S(2)}) collective-permute-start(bf16[72,1792]{1,0:T(8,128)(2,1)S(1)} %get-tuple-element.7), channel_id=1, source_target_pairs={{0,960},{64,0},{128,64},{192,128},{256,192},{320,256},{384,320},{4... | collective-permute-start | bytes 774152 | tf_op jit(solution)/shard_map/ppermute | solution.py:21
  110.2 1.9 collective-permute-done.7
  112.1 3.4 %collective-permute-start.8 = (bf16[72,3584]{1,0:T(8,128)(2,1)S(1)}, bf16[72,3584]{1,0:T(8,128)(2,1)S(1)}, u32[]{:S(2)}, u32[]{:S(2)}) collective-permute-start(bf16[72,3584]{1,0:T(8,128)(2,1)S(1)} %pad_maximum_fusion.2), channel_id=1, source_target_pairs={{0,64},{64,128},{128,192},{192,256},{256,320},{320,384},{384,448},... | collective-permute-start | bytes 1548296 | tf_op jit(solution)/shard_map/ppermute | solution.py:21
  116.0 2.5 %collective-permute-start.6 = (bf16[72,3584]{1,0:T(8,128)(2,1)S(1)}, bf16[72,3584]{1,0:T(8,128)(2,1)S(1)}, u32[]{:S(2)}, u32[]{:S(2)}) collective-permute-start(bf16[72,3584]{1,0:T(8,128)(2,1)S(1)} %pad_maximum_fusion.1), channel_id=1, source_target_pairs={{0,960},{64,0},{128,64},{192,128},{256,192},{320,256},{384,320},{4... | collective-permute-start | bytes 1548296 | tf_op jit(solution)/shard_map/ppermute | solution.py:21
  119.5 5.7 %collective-permute-done.8 = bf16[72,3584]{1,0:T(8,128)(2,1)S(1)} collective-permute-done((bf16[72,3584]{1,0:T(8,128)(2,1)S(1)}, bf16[72,3584]{1,0:T(8,128)(2,1)S(1)}, u32[]{:S(2)}, u32[]{:S(2)}) %collective-permute-start.8) | collective-permute-done | bytes 516128 | tf_op jit(solution)/shard_map/ppermute | solution.py:21
  125.1 5.1 %collective-permute-done.6 = bf16[72,3584]{1,0:T(8,128)(2,1)S(1)} collective-permute-done((bf16[72,3584]{1,0:T(8,128)(2,1)S(1)}, bf16[72,3584]{1,0:T(8,128)(2,1)S(1)}, u32[]{:S(2)}, u32[]{:S(2)}) %collective-permute-start.6) | collective-permute-done | bytes 516128 | tf_op jit(solution)/shard_map/ppermute | solution.py:21
  133.5 1.1 fusion.5
  134.6 6.7 %all-to-all-start.1 = ((bf16[4,72,896]{2,1,0:T(8,128)(2,1)}), bf16[4,72,896]{2,1,0:T(8,128)(2,1)S(1)}, u32[]{:S(2)}, u32[]{:S(2)}) async-start(bf16[4,72,896]{2,1,0:T(8,128)(2,1)} %bitcast.10), calls=%async_computation.1 | async-start | bytes 1032192 | tf_op jit(solution)/shard_map/all_to_all | solution.py:148
  141.4 25.0 %all-to-all-done.1 = bf16[4,72,896]{2,1,0:T(8,128)(2,1)S(1)} async-done(((bf16[4,72,896]{2,1,0:T(8,128)(2,1)}), bf16[4,72,896]{2,1,0:T(8,128)(2,1)S(1)}, u32[]{:S(2)}, u32[]{:S(2)}) %all-to-all-start.1) | async-done | bytes 516128 | tf_op jit(solution)/shard_map/all_to_all | solution.py:148
  167.1 1.9 collective-permute-start.9
  169.0 1.3 collective-permute-done.9
  170.9 24.1 %all_to_all.15 = bf16[32,8,1024]{2,1,0:T(8,128)(2,1)S(1)} all-to-all(bf16[32,8,1024]{2,1,0:T(8,128)(2,1)S(1)} %fusion.6), channel_id=1, replica_groups=mesh['za'=4,'zc'=4,'x'=4,'y'=8,'c'=2] {'x','y'}, dimensions={0} | all-to-all | bytes 1048576 | tf_op jit(solution)/shard_map/all_to_all | solution.py:164
  (111 shorter events, 21.4 us)
Async XLA Ops:
  0.6 77.0 %copy-start = (bf16[1,128,3584]{2,1,0:T(8,128)(2,1)S(1)}, bf16[1,128,3584]{2,1,0:T(8,128)(2,1)}, u32[]{:S(2)}) copy-start(bf16[1,128,3584]{2,1,0:T(8,128)(2,1)} %param.13) | copy-start | bytes 2752516
  0.6 0.9 copy-start.9
  2.4 26.4 %all-to-all-start = ((bf16[32,8,896]{2,1,0:T(8,128)(2,1)}), bf16[32,8,896]{2,1,0:T(8,128)(2,1)S(1)}, u32[]{:S(2)}, u32[]{:S(2)}) async-start(bf16[32,8,896]{2,1,0:T(8,128)(2,1)} %broadcast_in_dim.54), calls=%async_computation | async-start | bytes 917504 | tf_op jit(solution)/shard_map/all_to_all | solution.py:60
  12.7 0.7 copy-start.8
  13.4 0.7 copy-start.10
  29.2 3.2 %collective-permute-start = (bf16[72,896]{1,0:T(8,128)(2,1)S(1)}, bf16[72,896]{1,0:T(8,128)(2,1)S(1)}, u32[]{:S(2)}, u32[]{:S(2)}) collective-permute-start(bf16[72,896]{1,0:T(8,128)(2,1)S(1)} %slice.182), channel_id=1, source_target_pairs={{0,1},{1,0},{2,3},{3,2},{4,5},{5,4},{6,7},{7,6},{8,9},{9,8},{10,11... | collective-permute-start | bytes 387080 | tf_op jit(solution)/shard_map/ppermute | solution.py:25
  32.5 38.0 %copy-start.3 = (bf16[288,288]{1,0:T(8,128)(2,1)S(1)}, bf16[288,288]{1,0:T(8,128)(2,1)}, u32[]{:S(2)}) copy-start(bf16[288,288]{1,0:T(8,128)(2,1)} %constant.94.clone) | copy-start | bytes 497668
  70.9 6.1 %copy-start.1 = (bf16[1,3584,128]{2,1,0:T(8,128)(2,1)S(1)}, bf16[1,3584,128]{2,1,0:T(8,128)(2,1)}, u32[]{:S(2)}) copy-start(bf16[1,3584,128]{2,1,0:T(8,128)(2,1)} %param.11) | copy-start | bytes 2752516
  71.0 6.4 %copy-start.2 = (bf16[1,3584,128]{2,1,0:T(8,128)(2,1)S(1)}, bf16[1,3584,128]{2,1,0:T(8,128)(2,1)}, u32[]{:S(2)}) copy-start(bf16[1,3584,128]{2,1,0:T(8,128)(2,1)} %param.12) | copy-start | bytes 2752516
  71.0 15.8 %collective-permute-start.1 = (bf16[72,3584]{1,0:T(8,128)(2,1)S(1)}, bf16[72,3584]{1,0:T(8,128)(2,1)S(1)}, u32[]{:S(2)}, u32[]{:S(2)}) collective-permute-start(bf16[72,3584]{1,0:T(8,128)(2,1)S(1)} %pad_maximum_fusion), channel_id=1, source_target_pairs={{0,64},{64,128},{128,192},{192,256},{256,320},{320,384},{384,448},... | collective-permute-start | bytes 1548296 | tf_op jit(solution)/shard_map/ppermute | solution.py:21
  73.1 17.2 %collective-permute-start.3 = (bf16[72,3584]{1,0:T(8,128)(2,1)S(1)}, bf16[72,3584]{1,0:T(8,128)(2,1)S(1)}, u32[]{:S(2)}, u32[]{:S(2)}) collective-permute-start(bf16[72,3584]{1,0:T(8,128)(2,1)S(1)} %pad_maximum_fusion), channel_id=1, source_target_pairs={{0,960},{64,0},{128,64},{192,128},{256,192},{320,256},{384,320},{4... | collective-permute-start | bytes 1548296 | tf_op jit(solution)/shard_map/ppermute | solution.py:21
  86.9 10.6 %collective-permute-start.2 = (bf16[72,1792]{1,0:T(8,128)(2,1)S(1)}, bf16[72,1792]{1,0:T(8,128)(2,1)S(1)}, u32[]{:S(2)}, u32[]{:S(2)}) collective-permute-start(bf16[72,1792]{1,0:T(8,128)(2,1)S(1)} %slice.192), channel_id=1, source_target_pairs={{0,64},{64,128},{128,192},{192,256},{256,320},{320,384},{384,448},... | collective-permute-start | bytes 774152 | tf_op jit(solution)/shard_map/ppermute | solution.py:21
  90.3 10.5 %collective-permute-start.4 = (bf16[72,1792]{1,0:T(8,128)(2,1)S(1)}, bf16[72,1792]{1,0:T(8,128)(2,1)S(1)}, u32[]{:S(2)}, u32[]{:S(2)}) collective-permute-start(bf16[72,1792]{1,0:T(8,128)(2,1)S(1)} %slice.193), channel_id=1, source_target_pairs={{0,960},{64,0},{128,64},{192,128},{256,192},{320,256},{384,320},{4... | collective-permute-start | bytes 774152 | tf_op jit(solution)/shard_map/ppermute | solution.py:21
  103.6 8.4 %collective-permute-start.7 = (bf16[72,1792]{1,0:T(8,128)(2,1)S(1)}, bf16[72,1792]{1,0:T(8,128)(2,1)S(1)}, u32[]{:S(2)}, u32[]{:S(2)}) collective-permute-start(bf16[72,1792]{1,0:T(8,128)(2,1)S(1)} %get-tuple-element.8), channel_id=1, source_target_pairs={{0,64},{64,128},{128,192},{192,256},{256,320},{320,384},{384,448},... | collective-permute-start | bytes 774152 | tf_op jit(solution)/shard_map/ppermute | solution.py:21
  106.2 9.6 %collective-permute-start.5 = (bf16[72,1792]{1,0:T(8,128)(2,1)S(1)}, bf16[72,1792]{1,0:T(8,128)(2,1)S(1)}, u32[]{:S(2)}, u32[]{:S(2)}) collective-permute-start(bf16[72,1792]{1,0:T(8,128)(2,1)S(1)} %get-tuple-element.7), channel_id=1, source_target_pairs={{0,960},{64,0},{128,64},{192,128},{256,192},{320,256},{384,320},{4... | collective-permute-start | bytes 774152 | tf_op jit(solution)/shard_map/ppermute | solution.py:21
  112.1 13.0 %collective-permute-start.8 = (bf16[72,3584]{1,0:T(8,128)(2,1)S(1)}, bf16[72,3584]{1,0:T(8,128)(2,1)S(1)}, u32[]{:S(2)}, u32[]{:S(2)}) collective-permute-start(bf16[72,3584]{1,0:T(8,128)(2,1)S(1)} %pad_maximum_fusion.2), channel_id=1, source_target_pairs={{0,64},{64,128},{128,192},{192,256},{256,320},{320,384},{384,448},... | collective-permute-start | bytes 1548296 | tf_op jit(solution)/shard_map/ppermute | solution.py:21
  116.0 14.2 %collective-permute-start.6 = (bf16[72,3584]{1,0:T(8,128)(2,1)S(1)}, bf16[72,3584]{1,0:T(8,128)(2,1)S(1)}, u32[]{:S(2)}, u32[]{:S(2)}) collective-permute-start(bf16[72,3584]{1,0:T(8,128)(2,1)S(1)} %pad_maximum_fusion.1), channel_id=1, source_target_pairs={{0,960},{64,0},{128,64},{192,128},{256,192},{320,256},{384,320},{4... | collective-permute-start | bytes 1548296 | tf_op jit(solution)/shard_map/ppermute | solution.py:21
  130.2 0.8 copy-start.6
  131.0 0.8 copy-start.5
  131.8 0.8 copy-start.4
  132.7 0.8 copy-start.7
  134.6 31.8 %all-to-all-start.1 = ((bf16[4,72,896]{2,1,0:T(8,128)(2,1)}), bf16[4,72,896]{2,1,0:T(8,128)(2,1)S(1)}, u32[]{:S(2)}, u32[]{:S(2)}) async-start(bf16[4,72,896]{2,1,0:T(8,128)(2,1)} %bitcast.10), calls=%async_computation.1 | async-start | bytes 1032192 | tf_op jit(solution)/shard_map/all_to_all | solution.py:148
  167.1 3.3 %collective-permute-start.9 = (bf16[72,1024]{1,0:T(8,128)(2,1)S(1)}, bf16[72,1024]{1,0:T(8,128)(2,1)S(1)}, u32[]{:S(2)}, u32[]{:S(2)}) collective-permute-start(bf16[72,1024]{1,0:T(8,128)(2,1)S(1)} %pad_maximum_fusion.3), channel_id=1, source_target_pairs={{0,1},{1,0},{2,3},{3,2},{4,5},{5,4},{6,7},{7,6},{8,9},{9,8},{10,11... | collective-permute-start | bytes 442376 | tf_op jit(solution)/shard_map/ppermute | solution.py:25

commit v2 on v1

--- a/solution.py
+++ b/solution.py
@@ -2,6 +2,7 @@
 import jax.numpy as jnp
 import numpy as np
 from jax import lax
+from jax.experimental import pallas as pl
 from jax.sharding import Mesh, PartitionSpec as P
 
 F32 = jnp.float32
@@ -10,14 +11,14 @@
 QN = 4
 PIECES = 2 * QN
 PACK = PIECES * CAP
-ZA, ZC = 4, 4
+ZA, ZB, ZD = 4, 2, 2
 EXTRA = 128
-ZAXES = ("za", "zc")
+ZAXES = ("za", "zb", "zd")
 PLANE = ("x", "y")
 
 
 def shift_z(values, step):
-    n = ZA * ZC
+    n = ZA * ZB * ZD
     return lax.ppermute(values, ZAXES, [(i, (i + step) % n) for i in range(n)])
 
 
@@ -25,20 +26,62 @@
     return lax.ppermute(values, "c", [(0, 1), (1, 0)])
 
 
-def unpack_matrix():
-    rows = np.arange(ZA * PACK)
+def turn_matrices():
+    rows = np.arange(ZB * ZA * PACK)
     slot = rows % CAP
-    chunk = rows // CAP % ZA
+    za = rows // CAP % ZA
     half = rows // (CAP * ZA) % 2
-    piece = rows // (CAP * ZA * 2)
-    source = ((chunk * 2 + half) * QN + piece) * CAP + slot
-    matrix = np.zeros((ZA * PACK, ZA * PACK), np.float32)
-    matrix[rows, source] = 1
+    kind = rows // (CAP * ZA * 2) % ZB
+    piece = rows // (CAP * ZA * 2 * ZB)
+    matrix = np.zeros((2, ZB * ZA * PACK, ZB * ZA * PACK), np.float32)
+    for last in range(2):
+        zb = np.where(kind == 1, last, 1 - last)
+        source = (((za * ZB + zb) * 2 + half) * QN + piece) * CAP + slot
+        matrix[last, rows, source] = 1
     return matrix
 
 
 def dot(a, b, dims=((1,), (0,))):
     return lax.dot_general(a, b, (dims, ((), ())), preferred_element_type=F32)
+
+
+def spread_kernel(tokens, cotangent, out):
+    lanes = out.shape[2]
+    rows = [
+        ref[:, q * lanes : (q + 1) * lanes] for ref in (tokens, cotangent) for q in range(QN)
+    ]
+    out[...] = jnp.broadcast_to(jnp.concatenate(rows, axis=0)[None], out.shape)
+
+
+def pack_kernel(here, above, below, out):
+    lanes = out.shape[1]
+    group = here.shape[0]
+    row = lax.broadcasted_iota(jnp.int32, (ZA * PACK, group), 0)
+    col = lax.broadcasted_iota(jnp.int32, (ZA * PACK, group), 1)
+    source = (row // (QN * CAP) % 2 * ZA + row // PACK) * CAP + row % CAP
+    total = jnp.zeros(out.shape, F32)
+    for q in range(QN):
+        cols = slice(q * lanes, (q + 1) * lanes)
+        summed = here[:, cols].astype(F32) + above[:, cols].astype(F32)
+        summed = (summed + below[:, cols].astype(F32)).astype(BF16)
+        pick = ((source == col) & (row // CAP % QN == q)).astype(F32).astype(BF16)
+        total = total + dot(pick, summed)
+    out[...] = total.astype(BF16)
+
+
+def finish_kernel(mine, mixed, grad_tokens, grad_gates):
+    lanes = mixed.shape[1] // QN
+    topk = grad_gates.shape[1]
+    total = mine[0].astype(F32)
+    for chip in range(1, mine.shape[0]):
+        total = total + mine[chip].astype(F32)
+    for q in range(QN):
+        cols = slice(q * lanes, (q + 1) * lanes)
+        mixed[:, cols] = total[q : q + 1, :lanes].astype(BF16)
+        grad_tokens[:, cols] = total[QN + q : QN + q + 1, :lanes].astype(BF16)
+    grad_gates[...] = (
+        total[0:1, lanes : lanes + topk] + total[0:1, lanes + topk : lanes + 2 * topk]
+    )
 
 
 def local(tokens, expert_ids, gates, w_gate, w_up, w_down, cotangent):
@@ -53,10 +96,9 @@
     sibling = expert + 1 - 2 * core
     w_gate, w_up, w_down = w_gate[0], w_up[0], w_down[0]
 
-    payload = jnp.concatenate(
-        [tokens.reshape(QN, lanes), cotangent.reshape(QN, lanes)], axis=0
-    )
-    spread = jnp.broadcast_to(payload[None], (chips, PIECES, lanes))
+    spread = pl.pallas_call(
+        spread_kernel, out_shape=jax.ShapeDtypeStruct((chips, PIECES, lanes), BF16)
+    )(tokens, cotangent)
     gathered = lax.all_to_all(spread, PLANE, 0, 0, tiled=True).reshape(chips * PIECES, lanes)
 
     ids = expert_ids.T
@@ -87,41 +129,49 @@
     chosen = dot(choose, gathered).astype(BF16)
     packed = chosen[:PACK] + swap_core(chosen[PACK:])
 
-    turn = jnp.asarray(unpack_matrix(), BF16)
-    strided = lax.all_gather(packed, "za", axis=0).reshape(ZA * PACK, lanes)
-    turned = dot(turn, strided).astype(BF16)
-    group = turned.shape[0] // QN
-    here = jnp.concatenate([turned[q * group : (q + 1) * group] for q in range(QN)], axis=1)
-    below = shift_z(here, 1)
-    above = shift_z(here, -1)
-    far_left = shift_z(below[:, :half_width], 1)
-    far_right = shift_z(above[:, half_width:], -1)
-    far = jnp.concatenate([far_left, far_right], axis=1)
-    rows = group // 2
+    zb = lax.axis_index("zb").astype(jnp.int32)
+    zd = lax.axis_index("zd").astype(jnp.int32)
+    turns = jnp.asarray(turn_matrices(), BF16)
+    turn_own = lax.dynamic_index_in_dim(turns, zb, 0, keepdims=False)
+    turn_other = lax.dynamic_index_in_dim(turns, jnp.where(zd == 1, 1 - zb, zb), 0, keepdims=False)
+    same = lax.all_gather(packed, ("za", "zb"), axis=0, tiled=True)
+    middle = same.shape[0] // 2
+    from_below = shift_z(same[:middle], 1)
+    from_above = shift_z(same[middle:], -1)
+    group = ZA * 2 * CAP
+
+    def in_rows(turned):
+        turned = turned.astype(BF16)
+        return jnp.concatenate(
+            [turned[2 * q * group : 2 * (q + 1) * group] for q in range(QN)], axis=1
+        )
 
     def expert_terms(values):
-        gate_pre = dot(values, w_gate)[:rows]
-        up_pre = dot(values, w_up)[:rows]
-        grad_hid = dot(values, w_down, ((1,), (1,)))[rows:]
+        gate_pre = dot(values, w_gate).reshape(2, group, -1)[:, : group // 2]
+        up_pre = dot(values, w_up).reshape(2, group, -1)[:, : group // 2]
+        grad_hid = dot(values, w_down, ((1,), (1,))).reshape(2, group, -1)[:, group // 2 :]
         sig = jax.nn.sigmoid(gate_pre)
         hid = (gate_pre * sig * up_pre).astype(BF16)
         grad_gate = (grad_hid * up_pre * sig * (1.0 + gate_pre * (1.0 - sig))).astype(BF16)
         grad_up = (grad_hid * gate_pre * sig).astype(BF16)
         none = jnp.zeros_like(hid)
-        out = dot(jnp.concatenate([hid, none], axis=0), w_down)
-        out = out + dot(jnp.concatenate([none, grad_gate], axis=0), w_gate, ((1,), (1,)))
-        out = out + dot(jnp.concatenate([none, grad_up], axis=0), w_up, ((1,), (1,)))
+
+        def in_half(first, second):
+            return jnp.concatenate([first, second], axis=1).reshape(2 * group, -1)
+
+        out = dot(in_half(hid, none), w_down)
+        out = out + dot(in_half(none, grad_gate), w_gate, ((1,), (1,)))
+        out = out + dot(in_half(none, grad_up), w_up, ((1,), (1,)))
         return out.astype(BF16)
 
-    terms_far = expert_terms(far)
-    terms_here, terms_below, terms_above = (
-        expert_terms(here),
-        expert_terms(below),
-        expert_terms(above),
-    )
+    terms_own = expert_terms(in_rows(dot(turn_own, same)))
+    terms_far, terms_here = terms_own[:group], terms_own[group:]
 
     back_left = shift_z(terms_far[:, :half_width], -1)
     back_right = shift_z(terms_far[:, half_width:], 1)
+    other = dot(turn_other[:, :middle], from_below) + dot(turn_other[:, middle:], from_above)
+    terms_other = expert_terms(in_rows(other))
+    terms_below, terms_above = terms_other[:group], terms_other[group:]
     low = jnp.concatenate(
         [
             (terms_below[:, :half_width].astype(F32) + back_left.astype(F32)).astype(BF16),
@@ -136,15 +186,9 @@
         ],
         axis=1,
     )
-    from_above = shift_z(low, -1)
-    from_below = shift_z(high, 1)
-    summed = (
-        terms_here.astype(F32) + from_above.astype(F32) + from_below.astype(F32)
-    ).astype(BF16)
-    stacked = jnp.concatenate(
-        [summed[:, q * lanes : (q + 1) * lanes] for q in range(QN)], axis=0
-    )
-    outgoing = dot(turn, stacked, ((0,), (0,))).astype(BF16).reshape(ZA, PACK, lanes)
+    outgoing = pl.pallas_call(
+        pack_kernel, out_shape=jax.ShapeDtypeStruct((ZA * PACK, lanes), BF16)
+    )(terms_here, shift_z(low, -1), shift_z(high, 1)).reshape(ZA, PACK, lanes)
     arrived = lax.all_to_all(outgoing, "za", 0, 0, tiled=True)
     results = jnp.sum(arrived.astype(F32), axis=0)
 
@@ -162,15 +206,18 @@
     dense = dot(choose, both, ((0,), (0,))).astype(BF16)
     dense = dense.reshape(chips, PIECES, lanes + EXTRA)
     mine = lax.all_to_all(dense, PLANE, 0, 0, tiled=True)
-    total = jnp.sum(mine.astype(F32), axis=0)
-    mixed = total[:QN, :lanes].astype(BF16).reshape(1, width)
-    grad_tokens = total[QN:, :lanes].astype(BF16).reshape(1, width)
-    grad_gates = total[0:1, lanes : lanes + topk] + total[0:1, lanes + topk : lanes + 2 * topk]
-    return mixed, grad_tokens, grad_gates
+    return pl.pallas_call(
+        finish_kernel,
+        out_shape=(
+            jax.ShapeDtypeStruct((1, width), BF16),
+            jax.ShapeDtypeStruct((1, width), BF16),
+            jax.ShapeDtypeStruct((1, topk), F32),
+        ),
+    )(mine)
 
 
 def solution(mesh, plane=(4, 8, 2)):
-    fine = Mesh(mesh.devices.reshape((ZA, ZC) + plane), ZAXES + PLANE + ("c",))
+    fine = Mesh(mesh.devices.reshape((ZA, ZB, ZD) + plane), ZAXES + PLANE + ("c",))
     rows = P(ZAXES + PLANE + ("c",), None)
     experts = PLANE + ("c",)
     return jax.shard_map(

time: 198 us -> 184 us (0.929)
  the two profiles are of different devices: /device:TPU:200 before, /device:TPU:8 now
where the time goes in v2:
time: 184 us; the launch traced here: 183 us
  blocking collectives  68.3 us (37%)
  starting transfers between devices  47.1 us (26%)
  waiting for transfers between devices  46 us (25%)
  matrix products  8.73 us (5%)
  Pallas kernels  6.47 us (4%)
  local copies, waits for them, and re-layouts  3.32 us (2%)
  other arithmetic  2.35 us (1%)
    all_gather x1, blocking collectives, local(): same = lax.all_gather(packed, ('za', 'zb'), axis=0, tiled=True)  43.8 us
    all_to_all x1, blocking collectives, local(): mine = lax.all_to_all(dense, PLANE, 0, 0, tiled=True)  24.5 us
    all_to_all x1, waiting for transfers between devices, local(): arrived = lax.all_to_all(outgoing, 'za', 0, 0, tiled=True)  20.2 us
    ppermute x6, starting transfers between devices, shift_z(): return lax.ppermute(values, ZAXES, [(i, (i + step) % n) for i in range(n)])  20 us
    all_to_all x1, starting transfers between devices, local(): lax.all_to_all(spread, PLANE, 0, 0, tiled=True)  16.6 us
    ppermute x6, waiting for transfers between devices, shift_z(): return lax.ppermute(values, ZAXES, [(i, (i + step) % n) for i in range(n)])  12.1 us
    all_to_all x1, waiting for transfers between devices, local(): lax.all_to_all(spread, PLANE, 0, 0, tiled=True)  11.2 us
    dot_general x20, matrix products, dot(): return lax.dot_general(a, b, (dims, ((), ())), preferred_element_type=F32)  8.73 us
  transfers between devices with their start and end apart: 10, of which 7 were waited for; matrix products, arithmetic and copies ran while one was open for 5% of the time, Pallas kernels for 0%

profile of v2, /device:TPU:8, one launch (start us, length us, event | category | flops | bytes accessed | tf_op | source)
XLA Modules:
  0.0 183.5 jit_solution(8205227730993898738)
XLA Ops:
  0.7 1.7 shard_map.103
  2.4 16.6 %all-to-all-start = ((bf16[32,8,896]{2,1,0:T(8,128)(2,1)}), bf16[32,8,896]{2,1,0:T(8,128)(2,1)S(1)}, u32[]{:S(2)}, u32[]{:S(2)}) async-start(bf16[32,8,896]{2,1,0:T(8,128)(2,1)} %shard_map.103), calls=%async_computation | async-start | bytes 917504 | tf_op jit(solution)/shard_map/all_to_all | solution.py:102
  20.8 11.2 %all-to-all-done = bf16[32,8,896]{2,1,0:T(8,128)(2,1)S(1)} async-done(((bf16[32,8,896]{2,1,0:T(8,128)(2,1)}), bf16[32,8,896]{2,1,0:T(8,128)(2,1)S(1)}, u32[]{:S(2)}, u32[]{:S(2)}) %all-to-all-start) | async-done | bytes 458784 | tf_op jit(solution)/shard_map/all_to_all | solution.py:102
  32.4 1.9 %collective-permute-start = (bf16[72,896]{1,0:T(8,128)(2,1)S(1)}, bf16[72,896]{1,0:T(8,128)(2,1)S(1)}, u32[]{:S(2)}, u32[]{:S(2)}) collective-permute-start(bf16[72,896]{1,0:T(8,128)(2,1)S(1)} %slice.151), channel_id=1, source_target_pairs={{0,1},{1,0},{2,3},{3,2},{4,5},{5,4},{6,7},{7,6},{8,9},{9,8},{10,11... | collective-permute-start | bytes 387080 | tf_op jit(solution)/shard_map/ppermute | solution.py:26
  34.4 1.2 collective-permute-done
  35.7 43.8 %all_gather.3 = bf16[576,896]{1,0:T(8,128)(2,1)S(1)} all-gather(bf16[72,896]{1,0:T(8,128)(2,1)S(1)} %slice_add_fusion), channel_id=1, replica_groups=mesh['za'=4,'zb'=2,'zd'=2,'x'=4,'y'=8,'c'=2] {'za','zb'}, dimensions={0}, use_global_device_ids=true | all-gather | bytes 1161216 | tf_op jit(solution)/shard_map/all_gather | solution.py:137
  79.6 1.0 convolution_convert_fusion
  80.8 1.0 copy-done.1
  83.1 3.0 %collective-permute-start.1 = (bf16[288,896]{1,0:T(8,128)(2,1)S(1)}, bf16[288,896]{1,0:T(8,128)(2,1)S(1)}, u32[]{:S(2)}, u32[]{:S(2)}) collective-permute-start(bf16[288,896]{1,0:T(8,128)(2,1)S(1)} %get-tuple-element.17), channel_id=1, source_target_pairs={{0,64},{64,128},{128,192},{192,256},{256,320},{320,384},{384,448},... | collective-permute-start | bytes 1548296 | tf_op jit(solution)/shard_map/ppermute | solution.py:22
  86.1 4.0 %collective-permute-start.2 = (bf16[288,896]{1,0:T(8,128)(2,1)S(1)}, bf16[288,896]{1,0:T(8,128)(2,1)S(1)}, u32[]{:S(2)}, u32[]{:S(2)}) collective-permute-start(bf16[288,896]{1,0:T(8,128)(2,1)S(1)} %get-tuple-element.18), channel_id=1, source_target_pairs={{0,960},{64,0},{128,64},{192,128},{256,192},{320,256},{384,320},{4... | collective-permute-start | bytes 1548296 | tf_op jit(solution)/shard_map/ppermute | solution.py:22
  91.5 2.8 %collective-permute-start.5 = (bf16[72,1792]{1,0:T(8,128)(2,1)S(1)}, bf16[72,1792]{1,0:T(8,128)(2,1)S(1)}, u32[]{:S(2)}, u32[]{:S(2)}) collective-permute-start(bf16[72,1792]{1,0:T(8,128)(2,1)S(1)} %get-tuple-element.11), channel_id=1, source_target_pairs={{0,64},{64,128},{128,192},{192,256},{256,320},{320,384},{384,448},... | collective-permute-start | bytes 774152 | tf_op jit(solution)/shard_map/ppermute | solution.py:22
  94.3 4.2 %collective-permute-start.3 = (bf16[72,1792]{1,0:T(8,128)(2,1)S(1)}, bf16[72,1792]{1,0:T(8,128)(2,1)S(1)}, u32[]{:S(2)}, u32[]{:S(2)}) collective-permute-start(bf16[72,1792]{1,0:T(8,128)(2,1)S(1)} %get-tuple-element.12), channel_id=1, source_target_pairs={{0,960},{64,0},{128,64},{192,128},{256,192},{320,256},{384,320},{4... | collective-permute-start | bytes 774152 | tf_op jit(solution)/shard_map/ppermute | solution.py:22
  98.5 2.6 %collective-permute-done.2 = bf16[288,896]{1,0:T(8,128)(2,1)S(1)} collective-permute-done((bf16[288,896]{1,0:T(8,128)(2,1)S(1)}, bf16[288,896]{1,0:T(8,128)(2,1)S(1)}, u32[]{:S(2)}, u32[]{:S(2)}) %collective-permute-start.2) | collective-permute-done | bytes 516128 | tf_op jit(solution)/shard_map/ppermute | solution.py:22
  105.7 3.9 %collective-permute-start.4 = (bf16[72,3584]{1,0:T(8,128)(2,1)S(1)}, bf16[72,3584]{1,0:T(8,128)(2,1)S(1)}, u32[]{:S(2)}, u32[]{:S(2)}) collective-permute-start(bf16[72,3584]{1,0:T(8,128)(2,1)S(1)} %pad_maximum_fusion.2), channel_id=1, source_target_pairs={{0,960},{64,0},{128,64},{192,128},{256,192},{320,256},{384,320},{4... | collective-permute-start | bytes 1548296 | tf_op jit(solution)/shard_map/ppermute | solution.py:22
  109.7 1.9 %collective-permute-start.6 = (bf16[72,3584]{1,0:T(8,128)(2,1)S(1)}, bf16[72,3584]{1,0:T(8,128)(2,1)S(1)}, u32[]{:S(2)}, u32[]{:S(2)}) collective-permute-start(bf16[72,3584]{1,0:T(8,128)(2,1)S(1)} %pad_maximum_fusion.3), channel_id=1, source_target_pairs={{0,64},{64,128},{128,192},{192,256},{256,320},{320,384},{384,448},... | collective-permute-start | bytes 1548296 | tf_op jit(solution)/shard_map/ppermute | solution.py:22
  112.4 4.3 %collective-permute-done.4.above = bf16[72,3584]{1,0:T(8,128)(2,1)S(1)} collective-permute-done((bf16[72,3584]{1,0:T(8,128)(2,1)S(1)}, bf16[72,3584]{1,0:T(8,128)(2,1)S(1)}, u32[]{:S(2)}, u32[]{:S(2)}) %collective-permute-start.4) | collective-permute-done | bytes 516128 | tf_op jit(solution)/shard_map/ppermute | solution.py:22
  116.7 5.2 %collective-permute-done.6.below = bf16[72,3584]{1,0:T(8,128)(2,1)S(1)} collective-permute-done((bf16[72,3584]{1,0:T(8,128)(2,1)S(1)}, bf16[72,3584]{1,0:T(8,128)(2,1)S(1)}, u32[]{:S(2)}, u32[]{:S(2)}) %collective-permute-start.6) | collective-permute-done | bytes 516128 | tf_op jit(solution)/shard_map/ppermute | solution.py:22
  122.7 3.0 %shard_map.104 = bf16[288,896]{1,0:T(8,128)(2,1)} custom-call(bf16[72,3584]{1,0:T(8,128)(2,1)} %slice.158.here, bf16[72,3584]{1,0:T(8,128)(2,1)} %copy-done.3, bf16[72,3584]{1,0:T(8,128)(2,1)} %copy-done.4), custom_call_target="tpu_custom_call" | custom-call | tf_op jit(solution)/shard_map/pallas_call | solution.py:189
  125.7 6.7 %all-to-all-start.1 = ((bf16[4,72,896]{2,1,0:T(8,128)(2,1)}), bf16[4,72,896]{2,1,0:T(8,128)(2,1)S(1)}, u32[]{:S(2)}, u32[]{:S(2)}) async-start(bf16[4,72,896]{2,1,0:T(8,128)(2,1)} %bitcast.75), calls=%async_computation.1 | async-start | bytes 1032192 | tf_op jit(solution)/shard_map/all_to_all | solution.py:192
  132.5 20.2 %all-to-all-done.1 = bf16[4,72,896]{2,1,0:T(8,128)(2,1)S(1)} async-done(((bf16[4,72,896]{2,1,0:T(8,128)(2,1)}), bf16[4,72,896]{2,1,0:T(8,128)(2,1)S(1)}, u32[]{:S(2)}, u32[]{:S(2)}) %all-to-all-start.1) | async-done | bytes 516128 | tf_op jit(solution)/shard_map/all_to_all | solution.py:192
  153.4 1.9 %collective-permute-start.7 = (bf16[72,1024]{1,0:T(8,128)(2,1)S(1)}, bf16[72,1024]{1,0:T(8,128)(2,1)S(1)}, u32[]{:S(2)}, u32[]{:S(2)}) collective-permute-start(bf16[72,1024]{1,0:T(8,128)(2,1)S(1)} %pad_maximum_fusion.4), channel_id=1, source_target_pairs={{0,1},{1,0},{2,3},{3,2},{4,5},{5,4},{6,7},{7,6},{8,9},{9,8},{10,11... | collective-permute-start | bytes 442376 | tf_op jit(solution)/shard_map/ppermute | solution.py:26
  155.4 1.3 collective-permute-done.7
  157.2 24.5 %all_to_all.15.mine = bf16[32,8,1024]{2,1,0:T(8,128)(2,1)} all-to-all(bf16[32,8,1024]{2,1,0:T(8,128)(2,1)S(1)} %fusion.2), channel_id=1, replica_groups=mesh['za'=4,'zb'=2,'zd'=2,'x'=4,'y'=8,'c'=2] {'x','y'}, dimensions={0} | all-to-all | bytes 1048576 | tf_op jit(solution)/shard_map/all_to_all | solution.py:208
  181.7 1.7 shard_map.105
  (79 shorter events, 12.4 us)
Async XLA Ops:
  0.6 81.9 %copy-start = (bf16[1,128,3584]{2,1,0:T(8,128)(2,1)S(1)}, bf16[1,128,3584]{2,1,0:T(8,128)(2,1)}, u32[]{:S(2)}) copy-start(bf16[1,128,3584]{2,1,0:T(8,128)(2,1)} %param.13) | copy-start | bytes 2752516
  0.6 33.7 %copy-start.5 = (bf16[2,576,576]{2,1,0:T(8,128)(2,1)S(1)}, bf16[2,576,576]{2,1,0:T(8,128)(2,1)}, u32[]{:S(2)}) copy-start(bf16[2,576,576]{2,1,0:T(8,128)(2,1)} %constant.107.clone) | copy-start | bytes 3981316
  2.4 29.6 %all-to-all-start = ((bf16[32,8,896]{2,1,0:T(8,128)(2,1)}), bf16[32,8,896]{2,1,0:T(8,128)(2,1)S(1)}, u32[]{:S(2)}, u32[]{:S(2)}) async-start(bf16[32,8,896]{2,1,0:T(8,128)(2,1)} %shard_map.103), calls=%async_computation | async-start | bytes 917504 | tf_op jit(solution)/shard_map/all_to_all | solution.py:102
  32.4 3.2 %collective-permute-start = (bf16[72,896]{1,0:T(8,128)(2,1)S(1)}, bf16[72,896]{1,0:T(8,128)(2,1)S(1)}, u32[]{:S(2)}, u32[]{:S(2)}) collective-permute-start(bf16[72,896]{1,0:T(8,128)(2,1)S(1)} %slice.151), channel_id=1, source_target_pairs={{0,1},{1,0},{2,3},{3,2},{4,5},{5,4},{6,7},{7,6},{8,9},{9,8},{10,11... | collective-permute-start | bytes 387080 | tf_op jit(solution)/shard_map/ppermute | solution.py:26
  80.6 1.2 copy-start.1
  80.7 1.4 copy-start.2
  83.1 18.9 %collective-permute-start.1 = (bf16[288,896]{1,0:T(8,128)(2,1)S(1)}, bf16[288,896]{1,0:T(8,128)(2,1)S(1)}, u32[]{:S(2)}, u32[]{:S(2)}) collective-permute-start(bf16[288,896]{1,0:T(8,128)(2,1)S(1)} %get-tuple-element.17), channel_id=1, source_target_pairs={{0,64},{64,128},{128,192},{192,256},{256,320},{320,384},{384,448},... | collective-permute-start | bytes 1548296 | tf_op jit(solution)/shard_map/ppermute | solution.py:22
  86.1 15.0 %collective-permute-start.2 = (bf16[288,896]{1,0:T(8,128)(2,1)S(1)}, bf16[288,896]{1,0:T(8,128)(2,1)S(1)}, u32[]{:S(2)}, u32[]{:S(2)}) collective-permute-start(bf16[288,896]{1,0:T(8,128)(2,1)S(1)} %get-tuple-element.18), channel_id=1, source_target_pairs={{0,960},{64,0},{128,64},{192,128},{256,192},{320,256},{384,320},{4... | collective-permute-start | bytes 1548296 | tf_op jit(solution)/shard_map/ppermute | solution.py:22
  91.5 14.0 %collective-permute-start.5 = (bf16[72,1792]{1,0:T(8,128)(2,1)S(1)}, bf16[72,1792]{1,0:T(8,128)(2,1)S(1)}, u32[]{:S(2)}, u32[]{:S(2)}) collective-permute-start(bf16[72,1792]{1,0:T(8,128)(2,1)S(1)} %get-tuple-element.11), channel_id=1, source_target_pairs={{0,64},{64,128},{128,192},{192,256},{256,320},{320,384},{384,448},... | collective-permute-start | bytes 774152 | tf_op jit(solution)/shard_map/ppermute | solution.py:22
  94.3 11.1 %collective-permute-start.3 = (bf16[72,1792]{1,0:T(8,128)(2,1)S(1)}, bf16[72,1792]{1,0:T(8,128)(2,1)S(1)}, u32[]{:S(2)}, u32[]{:S(2)}) collective-permute-start(bf16[72,1792]{1,0:T(8,128)(2,1)S(1)} %get-tuple-element.12), channel_id=1, source_target_pairs={{0,960},{64,0},{128,64},{192,128},{256,192},{320,256},{384,320},{4... | collective-permute-start | bytes 774152 | tf_op jit(solution)/shard_map/ppermute | solution.py:22
  105.7 11.0 %collective-permute-start.4 = (bf16[72,3584]{1,0:T(8,128)(2,1)S(1)}, bf16[72,3584]{1,0:T(8,128)(2,1)S(1)}, u32[]{:S(2)}, u32[]{:S(2)}) collective-permute-start(bf16[72,3584]{1,0:T(8,128)(2,1)S(1)} %pad_maximum_fusion.2), channel_id=1, source_target_pairs={{0,960},{64,0},{128,64},{192,128},{256,192},{320,256},{384,320},{4... | collective-permute-start | bytes 1548296 | tf_op jit(solution)/shard_map/ppermute | solution.py:22
  109.7 12.2 %collective-permute-start.6 = (bf16[72,3584]{1,0:T(8,128)(2,1)S(1)}, bf16[72,3584]{1,0:T(8,128)(2,1)S(1)}, u32[]{:S(2)}, u32[]{:S(2)}) collective-permute-start(bf16[72,3584]{1,0:T(8,128)(2,1)S(1)} %pad_maximum_fusion.3), channel_id=1, source_target_pairs={{0,64},{64,128},{128,192},{192,256},{256,320},{320,384},{384,448},... | collective-permute-start | bytes 1548296 | tf_op jit(solution)/shard_map/ppermute | solution.py:22
  116.7 5.2 %copy-start.3 = (bf16[72,3584]{1,0:T(8,128)(2,1)}, bf16[72,3584]{1,0:T(8,128)(2,1)S(1)}, u32[]{:S(2)}) copy-start(bf16[72,3584]{1,0:T(8,128)(2,1)S(1)} %collective-permute-done.4.above) | copy-start | bytes 1548292
  121.9 0.8 copy-start.4
  125.7 27.0 %all-to-all-start.1 = ((bf16[4,72,896]{2,1,0:T(8,128)(2,1)}), bf16[4,72,896]{2,1,0:T(8,128)(2,1)S(1)}, u32[]{:S(2)}, u32[]{:S(2)}) async-start(bf16[4,72,896]{2,1,0:T(8,128)(2,1)} %bitcast.75), calls=%async_computation.1 | async-start | bytes 1032192 | tf_op jit(solution)/shard_map/all_to_all | solution.py:192
  153.4 3.3 %collective-permute-start.7 = (bf16[72,1024]{1,0:T(8,128)(2,1)S(1)}, bf16[72,1024]{1,0:T(8,128)(2,1)S(1)}, u32[]{:S(2)}, u32[]{:S(2)}) collective-permute-start(bf16[72,1024]{1,0:T(8,128)(2,1)S(1)} %pad_maximum_fusion.4), channel_id=1, source_target_pairs={{0,1},{1,0},{2,3},{3,2},{4,5},{5,4},{6,7},{7,6},{8,9},{9,8},{10,11... | collective-permute-start | bytes 442376 | tf_op jit(solution)/shard_map/ppermute | solution.py:26

commit v3 on v2

--- a/solution.py
+++ b/solution.py
@@ -3,6 +3,7 @@
 import numpy as np
 from jax import lax
 from jax.experimental import pallas as pl
+from jax.experimental.pallas import tpu as pltpu
 from jax.sharding import Mesh, PartitionSpec as P
 
 F32 = jnp.float32
@@ -22,27 +23,25 @@
     return lax.ppermute(values, ZAXES, [(i, (i + step) % n) for i in range(n)])
 
 
-def swap_core(values):
-    return lax.ppermute(values, "c", [(0, 1), (1, 0)])
-
-
-def turn_matrices():
-    rows = np.arange(ZB * ZA * PACK)
-    slot = rows % CAP
-    za = rows // CAP % ZA
-    half = rows // (CAP * ZA) % 2
-    kind = rows // (CAP * ZA * 2) % ZB
-    piece = rows // (CAP * ZA * 2 * ZB)
-    matrix = np.zeros((2, ZB * ZA * PACK, ZB * ZA * PACK), np.float32)
-    for last in range(2):
-        zb = np.where(kind == 1, last, 1 - last)
-        source = (((za * ZB + zb) * 2 + half) * QN + piece) * CAP + slot
-        matrix[last, rows, source] = 1
-    return matrix
+def both_cores(values):
+    return lax.all_gather(values, "c", axis=0)
 
 
 def dot(a, b, dims=((1,), (0,))):
     return lax.dot_general(a, b, (dims, ((), ())), preferred_element_type=F32)
+
+
+def one_hot(mask):
+    return mask.astype(F32).astype(BF16)
+
+
+def vmem_call(body, out_shape, **kwargs):
+    return pl.pallas_call(
+        body,
+        out_shape=out_shape,
+        compiler_params=pltpu.CompilerParams(vmem_limit_bytes=16 * 2**20),
+        **kwargs,
+    )
 
 
 def spread_kernel(tokens, cotangent, out):
@@ -53,20 +52,57 @@
     out[...] = jnp.broadcast_to(jnp.concatenate(rows, axis=0)[None], out.shape)
 
 
-def pack_kernel(here, above, below, out):
+def expert_kernel(base, low, high, w_gate, w_up, w_down, *outs):
+    lanes = low.shape[1]
+    middle = low.shape[0]
+    count = base.shape[0]
+    first, second = outs[: len(outs) // 2 + len(outs) % 2], outs[-(len(outs) // 2) :]
+    spots = lax.broadcasted_iota(jnp.int32, (count, middle), 1)
+    gate_pre = up_pre = grad_hid = jnp.zeros((count, w_down.shape[0]), F32)
+    for q in range(QN):
+        cols = slice(q * lanes, (q + 1) * lanes)
+        rows = []
+        for half in range(2):
+            want = base[...] + (half * QN + q) * CAP
+            part = dot(one_hot(spots == want), low[...])
+            part = part + dot(one_hot(spots + middle == want), high[...])
+            rows.append(part.astype(BF16))
+        gate_pre = gate_pre + dot(rows[0], w_gate[cols, :])
+        up_pre = up_pre + dot(rows[0], w_up[cols, :])
+        grad_hid = grad_hid + dot(rows[1], w_down[:, cols], ((1,), (1,)))
+    sig = 1.0 / (1.0 + jnp.exp(-gate_pre))
+    hid = (gate_pre * sig * up_pre).astype(BF16)
+    grad_gate = (grad_hid * up_pre * sig * (1.0 + gate_pre * (1.0 - sig))).astype(BF16)
+    grad_up = (grad_hid * gate_pre * sig).astype(BF16)
+    row = lax.broadcasted_iota(jnp.int32, (count, count), 0)
+    col = lax.broadcasted_iota(jnp.int32, (count, count), 1)
+    for kind, refs in enumerate((first, second)):
+        at = col - kind * (count // 2)
+        upper = one_hot((row < count // 2) & (at == row))
+        lower = one_hot((row >= count // 2) & (at == row - count // 2))
+        hid_rows = dot(upper, hid).astype(BF16)
+        gate_rows = dot(lower, grad_gate).astype(BF16)
+        up_rows = dot(lower, grad_up).astype(BF16)
+        for q in range(QN):
+            cols = slice(q * lanes, (q + 1) * lanes)
+            term = dot(hid_rows, w_down[:, cols])
+            term = term + dot(gate_rows, w_gate[cols, :], ((1,), (1,)))
+            term = term + dot(up_rows, w_up[cols, :], ((1,), (1,)))
+            each = QN // len(refs)
+            refs[q // each][:, q % each * lanes : (q % each + 1) * lanes] = term.astype(BF16)
+
+
+def pack_kernel(source, here, above, below, out):
     lanes = out.shape[1]
-    group = here.shape[0]
-    row = lax.broadcasted_iota(jnp.int32, (ZA * PACK, group), 0)
-    col = lax.broadcasted_iota(jnp.int32, (ZA * PACK, group), 1)
-    source = (row // (QN * CAP) % 2 * ZA + row // PACK) * CAP + row % CAP
-    total = jnp.zeros(out.shape, F32)
+    count = out.shape[0]
+    parts = []
     for q in range(QN):
         cols = slice(q * lanes, (q + 1) * lanes)
         summed = here[:, cols].astype(F32) + above[:, cols].astype(F32)
-        summed = (summed + below[:, cols].astype(F32)).astype(BF16)
-        pick = ((source == col) & (row // CAP % QN == q)).astype(F32).astype(BF16)
-        total = total + dot(pick, summed)
-    out[...] = total.astype(BF16)
+        parts.append(summed + below[:, cols].astype(F32))
+    stacked = jnp.concatenate(parts, axis=0).astype(BF16)
+    spots = lax.broadcasted_iota(jnp.int32, (count, count), 1)
+    out[...] = dot(one_hot(spots == source[...]), stacked).astype(BF16)
 
 
 def finish_kernel(mine, mixed, grad_tokens, grad_gates):
@@ -127,51 +163,40 @@
     route_rows = dot(in_slot[:CAP].astype(BF16), named.astype(BF16), ((1,), (1,)))
 
     chosen = dot(choose, gathered).astype(BF16)
-    packed = chosen[:PACK] + swap_core(chosen[PACK:])
+    halves = both_cores(chosen[PACK:])
+    packed = chosen[:PACK] + jnp.where(core == 0, halves[1], halves[0])
 
     zb = lax.axis_index("zb").astype(jnp.int32)
     zd = lax.axis_index("zd").astype(jnp.int32)
-    turns = jnp.asarray(turn_matrices(), BF16)
-    turn_own = lax.dynamic_index_in_dim(turns, zb, 0, keepdims=False)
-    turn_other = lax.dynamic_index_in_dim(turns, jnp.where(zd == 1, 1 - zb, zb), 0, keepdims=False)
+    group = ZA * 2 * CAP
+    index = jnp.arange(group, dtype=jnp.int32)[:, None]
+
+    def base_of(last):
+        at = jnp.where(index < group // 2, 1 - last, last)
+        return (index // CAP % ZA * ZB + at) * PACK + index % CAP
+
     same = lax.all_gather(packed, ("za", "zb"), axis=0, tiled=True)
     middle = same.shape[0] // 2
     from_below = shift_z(same[:middle], 1)
     from_above = shift_z(same[middle:], -1)
-    group = ZA * 2 * CAP
-
-    def in_rows(turned):
-        turned = turned.astype(BF16)
-        return jnp.concatenate(
-            [turned[2 * q * group : 2 * (q + 1) * group] for q in range(QN)], axis=1
-        )
-
-    def expert_terms(values):
-        gate_pre = dot(values, w_gate).reshape(2, group, -1)[:, : group // 2]
-        up_pre = dot(values, w_up).reshape(2, group, -1)[:, : group // 2]
-        grad_hid = dot(values, w_down, ((1,), (1,))).reshape(2, group, -1)[:, group // 2 :]
-        sig = jax.nn.sigmoid(gate_pre)
-        hid = (gate_pre * sig * up_pre).astype(BF16)
-        grad_gate = (grad_hid * up_pre * sig * (1.0 + gate_pre * (1.0 - sig))).astype(BF16)
-        grad_up = (grad_hid * gate_pre * sig).astype(BF16)
-        none = jnp.zeros_like(hid)
-
-        def in_half(first, second):
-            return jnp.concatenate([first, second], axis=1).reshape(2 * group, -1)
-
-        out = dot(in_half(hid, none), w_down)
-        out = out + dot(in_half(none, grad_gate), w_gate, ((1,), (1,)))
-        out = out + dot(in_half(none, grad_up), w_up, ((1,), (1,)))
-        return out.astype(BF16)
-
-    terms_own = expert_terms(in_rows(dot(turn_own, same)))
-    terms_far, terms_here = terms_own[:group], terms_own[group:]
-
-    back_left = shift_z(terms_far[:, :half_width], -1)
-    back_right = shift_z(terms_far[:, half_width:], 1)
-    other = dot(turn_other[:, :middle], from_below) + dot(turn_other[:, middle:], from_above)
-    terms_other = expert_terms(in_rows(other))
-    terms_below, terms_above = terms_other[:group], terms_other[group:]
+
+    def expert_terms(last, lower, upper, splits):
+        width_of = [width // n for n in splits for _ in range(n)]
+        return vmem_call(
+            expert_kernel,
+            [jax.ShapeDtypeStruct((group, w), BF16) for w in width_of],
+            cost_estimate=pl.CostEstimate(
+                flops=36 * group * width * w_down.shape[0], bytes_accessed=12 * width * w_down.shape[0], transcendentals=0
+            ),
+        )(base_of(last), lower, upper, w_gate, w_up, w_down)
+
+    far_left, far_right, terms_here = expert_terms(zb, same[:middle], same[middle:], (2, 1))
+
+    back_left = shift_z(far_left, -1)
+    back_right = shift_z(far_right, 1)
+    terms_below, terms_above = expert_terms(
+        jnp.where(zd == 1, 1 - zb, zb), from_below, from_above, (1, 1)
+    )
     low = jnp.concatenate(
         [
             (terms_below[:, :half_width].astype(F32) + back_left.astype(F32)).astype(BF16),
@@ -186,9 +211,11 @@
         ],
         axis=1,
     )
-    outgoing = pl.pallas_call(
-        pack_kernel, out_shape=jax.ShapeDtypeStruct((ZA * PACK, lanes), BF16)
-    )(terms_here, shift_z(low, -1), shift_z(high, 1)).reshape(ZA, PACK, lanes)
+    row = jnp.arange(ZA * PACK, dtype=jnp.int32)[:, None]
+    source = (row // CAP % QN) * group + (row // (QN * CAP) % 2 * ZA + row // PACK) * CAP
+    outgoing = vmem_call(pack_kernel, jax.ShapeDtypeStruct((ZA * PACK, lanes), BF16))(
+        source + row % CAP, terms_here, shift_z(low, -1), shift_z(high, 1)
+    ).reshape(ZA, PACK, lanes)
     arrived = lax.all_to_all(outgoing, "za", 0, 0, tiled=True)
     results = jnp.sum(arrived.astype(F32), axis=0)
 
@@ -201,9 +228,11 @@
     carried = jnp.concatenate([dots_high * route_rows, dots_low * route_rows], axis=1)
     carried = jnp.pad(carried, ((0, PACK - CAP), (0, EXTRA - 2 * topk)))
     scaled = jnp.concatenate([results * gate_rows, carried], axis=1).astype(BF16)
-    both = jnp.concatenate([scaled, swap_core(scaled)], axis=0)
-
-    dense = dot(choose, both, ((0,), (0,))).astype(BF16)
+    both = both_cores(scaled).reshape(2 * PACK, lanes + EXTRA)
+    swapped = jnp.concatenate([choose[PACK:], choose[:PACK]], axis=0)
+    choose_back = jnp.where(core == 0, choose, swapped)
+
+    dense = dot(choose_back, both, ((0,), (0,))).astype(BF16)
     dense = dense.reshape(chips, PIECES, lanes + EXTRA)
     mine = lax.all_to_all(dense, PLANE, 0, 0, tiled=True)
     return pl.pallas_call(

time: 184 us -> 181 us (0.984)
  Pallas kernels: 6.47 us -> 15 us
  matrix products: 8.73 us -> 1.3 us
  waiting for transfers between devices: 46 us -> 38.7 us
  local copies, waits for them, and re-layouts: 3.32 us -> 6.4 us
  blocking collectives: 68.3 us -> 70.5 us
  starting transfers between devices: 47.1 us -> 45.1 us
    pallas_call x1 -> x3, Pallas kernels: 3.04 us -> 11.8 us  [the longest x2 10.4 us: expert_terms(): vmem_call(expert_kernel, [jax.ShapeDtypeStruct((group, w), BF16) for w in...]
    dot_general x20 -> x5, matrix products: 8.73 us -> 1.3 us  [dot(): return lax.dot_general(a, b, (dims, ((), ())), preferred_element_type=F32)]
    ppermute x6, waiting for transfers between devices: 12.1 us -> 6.39 us  [shift_z(): return lax.ppermute(values, ZAXES, [(i, (i + step) % n) for i in range(n)])]
    unnamed x13 -> x34, local copies, waits for them, and re-layouts: 1.92 us -> 6.17 us
    all_gather x0 -> x2, blocking collectives: none -> 4.01 us  [both_cores(): return lax.all_gather(values, 'c', axis=0)]
    ppermute x2 -> x0, starting transfers between devices: 3.84 us -> none  [swap_core(): return lax.ppermute(values, 'c', [(0, 1), (1, 0)])]
    ppermute x2 -> x0, waiting for transfers between devices: 2.56 us -> none  [swap_core(): return lax.ppermute(values, 'c', [(0, 1), (1, 0)])]
  transfers between devices with their start and end apart: 10 -> 8, of which waited for: 7 -> 4; matrix products, arithmetic and copies ran while one was open for 5% -> 1% of each run, Pallas kernels for 0% -> 6%
where the time goes in v3:
time: 181 us; the launch traced here: 180 us
  blocking collectives  70.5 us (39%)
  starting transfers between devices  45.1 us (25%)
  waiting for transfers between devices  38.7 us (21%)
  Pallas kernels  15 us (8%)
  local copies, waits for them, and re-layouts  6.4 us (4%)
  other arithmetic  2.33 us (1%)
    all_gather x1, blocking collectives, local(): same = lax.all_gather(packed, ('za', 'zb'), axis=0, tiled=True)  43.6 us
    all_to_all x1, blocking collectives, local(): mine = lax.all_to_all(dense, PLANE, 0, 0, tiled=True)  22.9 us
    all_to_all x1, waiting for transfers between devices, local(): arrived = lax.all_to_all(outgoing, 'za', 0, 0, tiled=True)  21.6 us
    ppermute x6, starting transfers between devices, shift_z(): return lax.ppermute(values, ZAXES, [(i, (i + step) % n) for i in range(n)])  21.3 us
    all_to_all x1, starting transfers between devices, local(): lax.all_to_all(spread, PLANE, 0, 0, tiled=True)  16.6 us
    all_to_all x1, waiting for transfers between devices, local(): lax.all_to_all(spread, PLANE, 0, 0, tiled=True)  10.7 us
    pallas_call x2, Pallas kernels, expert_terms(): vmem_call(expert_kernel, [jax.ShapeDtypeStruct((group, w), BF16) for w in...  10.4 us
    all_to_all x1, starting transfers between devices, local(): arrived = lax.all_to_all(outgoing, 'za', 0, 0, tiled=True)  7.19 us
  transfers between devices with their start and end apart: 8, of which 4 were waited for; matrix products, arithmetic and copies ran while one was open for 1% of the time, Pallas kernels for 6%

profile of v3, /device:TPU:8, one launch (start us, length us, event | category | flops | bytes accessed | tf_op | source)
XLA Modules:
  0.0 180.4 jit_solution(40478298535628279)
XLA Ops:
  0.6 1.5 shard_map.94
  2.2 16.6 %all-to-all-start = ((bf16[32,8,896]{2,1,0:T(8,128)(2,1)}), bf16[32,8,896]{2,1,0:T(8,128)(2,1)S(1)}, u32[]{:S(2)}, u32[]{:S(2)}) async-start(bf16[32,8,896]{2,1,0:T(8,128)(2,1)} %shard_map.94), calls=%async_computation | async-start | bytes 917504 | tf_op jit(solution)/shard_map/all_to_all | solution.py:138
  21.2 10.7 %all-to-all-done = bf16[32,8,896]{2,1,0:T(8,128)(2,1)S(1)} async-done(((bf16[32,8,896]{2,1,0:T(8,128)(2,1)}), bf16[32,8,896]{2,1,0:T(8,128)(2,1)S(1)}, u32[]{:S(2)}, u32[]{:S(2)}) %all-to-all-start) | async-done | bytes 458784 | tf_op jit(solution)/shard_map/all_to_all | solution.py:138
  32.2 2.0 %all-gather = bf16[144,896]{1,0:T(8,128)(2,1)S(1)} all-gather(bf16[72,896]{1,0:T(8,128)(2,1)S(1)} %slice.82), channel_id=2, replica_groups=mesh['za'=4,'zb'=2,'zd'=2,'x'=4,'y'=8,'c'=2] {'c'}, dimensions={0}, use_global_device_ids=true | all-gather | bytes 387072 | tf_op jit(solution)/shard_map/all_gather | solution.py:27
  34.3 43.6 %all_gather.15 = bf16[576,896]{1,0:T(8,128)(2,1)S(1)} all-gather(bf16[72,896]{1,0:T(8,128)(2,1)S(1)} %fusion.26), channel_id=1, replica_groups=mesh['za'=4,'zb'=2,'zd'=2,'x'=4,'y'=8,'c'=2] {'za','zb'}, dimensions={0}, use_global_device_ids=true | all-gather | bytes 1161216 | tf_op jit(solution)/shard_map/all_gather | solution.py:178
  78.0 3.6 %collective-permute-start = (bf16[288,896]{1,0:T(8,128)(2,1)S(1)}, bf16[288,896]{1,0:T(8,128)(2,1)}, u32[]{:S(2)}, u32[]{:S(2)}) collective-permute-start(bf16[288,896]{1,0:T(8,128)(2,1)S(1)} %get-tuple-element.18.low), channel_id=1, source_target_pairs={{0,64},{64,128},{128,192},{192,256},{256,320},{320,384},{384,448},... | collective-permute-start | bytes 1548296 | tf_op jit(solution)/shard_map/ppermute | solution.py:23
  81.6 3.6 %collective-permute-start.1 = (bf16[288,896]{1,0:T(8,128)(2,1)S(1)}, bf16[288,896]{1,0:T(8,128)(2,1)}, u32[]{:S(2)}, u32[]{:S(2)}) collective-permute-start(bf16[288,896]{1,0:T(8,128)(2,1)S(1)} %get-tuple-element.17.high), channel_id=1, source_target_pairs={{0,960},{64,0},{128,64},{192,128},{256,192},{320,256},{384,320},{4... | collective-permute-start | bytes 1548296 | tf_op jit(solution)/shard_map/ppermute | solution.py:23
  85.2 1.2 copy-done.2
  86.4 4.6 %shard_map.95 = (bf16[72,1792]{1,0:T(8,128)(2,1)S(1)}, bf16[72,1792]{1,0:T(8,128)(2,1)}, bf16[72,3584]{1,0:T(8,128)(2,1)S(1)}) custom-call(s32[72,1]{1,0:T(8,128)S(1)} %fusion.40.base, bf16[288,896]{1,0:T(8,128)(2,1)S(1)} %get-tuple-element.18.low, bf16[288,896]{1,0:T(8,128)(2,1)S(1)} %get-tuple-element.17.high, bf16[3584,128]{1,0:T(8,128)(2,1)S(1)} %bitcast.22, ...), custom_call_target="tpu_custom_call" | custom-call | flops 1189085184 | bytes 5505024 | tf_op jit(solution)/shard_map/pallas_call | solution.py:185
  91.8 2.8 %collective-permute-start.4 = (bf16[72,1792]{1,0:T(8,128)(2,1)}, bf16[72,1792]{1,0:T(8,128)(2,1)}, u32[]{:S(2)}, u32[]{:S(2)}) collective-permute-start(bf16[72,1792]{1,0:T(8,128)(2,1)} %get-tuple-element.12), channel_id=1, source_target_pairs={{0,64},{64,128},{128,192},{192,256},{256,320},{320,384},{384,448},... | collective-permute-start | bytes 774152 | tf_op jit(solution)/shard_map/ppermute | solution.py:23
  94.6 4.2 %collective-permute-start.2 = (bf16[72,1792]{1,0:T(8,128)(2,1)}, bf16[72,1792]{1,0:T(8,128)(2,1)S(1)}, u32[]{:S(2)}, u32[]{:S(2)}) collective-permute-start(bf16[72,1792]{1,0:T(8,128)(2,1)} %copy-done.4), channel_id=1, source_target_pairs={{0,960},{64,0},{128,64},{192,128},{256,192},{320,256},{384,320},{4... | collective-permute-start | bytes 774152 | tf_op jit(solution)/shard_map/ppermute | solution.py:23
  98.9 1.2 copy-done.3
  100.1 5.8 %shard_map.96 = (bf16[72,3584]{1,0:T(8,128)(2,1)S(1)}, bf16[72,3584]{1,0:T(8,128)(2,1)S(1)}) custom-call(s32[72,1]{1,0:T(8,128)S(1)} %fusion.39.base, bf16[288,896]{1,0:T(8,128)(2,1)} %collective-permute-done.low, bf16[288,896]{1,0:T(8,128)(2,1)} %collective-permute-done.1.high, bf16[3584,128]{1,0:T(8,128)(2,1)S(1)} %bitcast.23, ...), custom_call_target="tpu_custom_call" | custom-call | flops 1189085184 | bytes 5505024 | tf_op jit(solution)/shard_map/pallas_call | solution.py:185
  105.9 1.0 add_convert_fusion
  107.0 1.9 %collective-permute-start.5 = (bf16[72,3584]{1,0:T(8,128)(2,1)S(1)}, bf16[72,3584]{1,0:T(8,128)(2,1)S(1)}, u32[]{:S(2)}, u32[]{:S(2)}) collective-permute-start(bf16[72,3584]{1,0:T(8,128)(2,1)S(1)} %pad_maximum_fusion.1), channel_id=1, source_target_pairs={{0,64},{64,128},{128,192},{192,256},{256,320},{320,384},{384,448},... | collective-permute-start | bytes 1548296 | tf_op jit(solution)/shard_map/ppermute | solution.py:23
  109.0 5.1 %collective-permute-start.3 = (bf16[72,3584]{1,0:T(8,128)(2,1)S(1)}, bf16[72,3584]{1,0:T(8,128)(2,1)S(1)}, u32[]{:S(2)}, u32[]{:S(2)}) collective-permute-start(bf16[72,3584]{1,0:T(8,128)(2,1)S(1)} %pad_maximum_fusion), channel_id=1, source_target_pairs={{0,960},{64,0},{128,64},{192,128},{256,192},{320,256},{384,320},{4... | collective-permute-start | bytes 1548296 | tf_op jit(solution)/shard_map/ppermute | solution.py:23
  114.4 4.8 %collective-permute-done.5.below = bf16[72,3584]{1,0:T(8,128)(2,1)S(1)} collective-permute-done((bf16[72,3584]{1,0:T(8,128)(2,1)S(1)}, bf16[72,3584]{1,0:T(8,128)(2,1)S(1)}, u32[]{:S(2)}, u32[]{:S(2)}) %collective-permute-start.5) | collective-permute-done | bytes 516128 | tf_op jit(solution)/shard_map/ppermute | solution.py:23
  119.1 1.6 collective-permute-done.3.above
  120.8 1.3 shard_map.97
  122.1 7.2 %all-to-all-start.1 = ((bf16[4,72,896]{2,1,0:T(8,128)(2,1)}), bf16[4,72,896]{2,1,0:T(8,128)(2,1)S(1)}, u32[]{:S(2)}, u32[]{:S(2)}) async-start(bf16[4,72,896]{2,1,0:T(8,128)(2,1)} %bitcast.8), calls=%async_computation.1 | async-start | bytes 1032192 | tf_op jit(solution)/shard_map/all_to_all | solution.py:219
  130.9 21.6 %all-to-all-done.1 = bf16[4,72,896]{2,1,0:T(8,128)(2,1)S(1)} async-done(((bf16[4,72,896]{2,1,0:T(8,128)(2,1)}), bf16[4,72,896]{2,1,0:T(8,128)(2,1)S(1)}, u32[]{:S(2)}, u32[]{:S(2)}) %all-to-all-start.1) | async-done | bytes 516128 | tf_op jit(solution)/shard_map/all_to_all | solution.py:219
  153.2 2.0 %all_gather.16 = bf16[2,72,1024]{2,1,0:T(8,128)(2,1)S(1)} all-gather(bf16[1,72,1024]{2,1,0:T(8,128)(2,1)S(1)} %pad_maximum_fusion.2), channel_id=1, replica_groups=mesh['za'=4,'zb'=2,'zd'=2,'x'=4,'y'=8,'c'=2] {'c'}, dimensions={0}, use_global_device_ids=true | all-gather | bytes 442368 | tf_op jit(solution)/shard_map/all_gather | solution.py:27
  155.8 22.9 %all_to_all.15.mine = bf16[32,8,1024]{2,1,0:T(8,128)(2,1)} all-to-all(bf16[32,8,1024]{2,1,0:T(8,128)(2,1)S(1)} %fusion), channel_id=1, replica_groups=mesh['za'=4,'zb'=2,'zd'=2,'x'=4,'y'=8,'c'=2] {'x','y'}, dimensions={0} | all-to-all | bytes 1048576 | tf_op jit(solution)/shard_map/all_to_all | solution.py:237
  178.6 1.7 shard_map.98
  (78 shorter events, 6.7 us)
Async XLA Ops:
  2.2 29.6 %all-to-all-start = ((bf16[32,8,896]{2,1,0:T(8,128)(2,1)}), bf16[32,8,896]{2,1,0:T(8,128)(2,1)S(1)}, u32[]{:S(2)}, u32[]{:S(2)}) async-start(bf16[32,8,896]{2,1,0:T(8,128)(2,1)} %shard_map.94), calls=%async_computation | async-start | bytes 917504 | tf_op jit(solution)/shard_map/all_to_all | solution.py:138
  18.9 13.0 %copy-start.7 = (pred[144]{0:T(512)(128)(4,1)}, pred[144]{0:T(512)(128)(4,1)S(1)}, u32[]{:S(2)}) copy-start(pred[144]{0:T(512)(128)(4,1)S(1)} %get-tuple-element.31) | copy-start | bytes 436
  18.9 12.9 %copy-start.9 = (pred[144]{0:T(512)(128)(4,1)}, pred[144]{0:T(512)(128)(4,1)S(1)}, u32[]{:S(2)}) copy-start(pred[144]{0:T(512)(128)(4,1)S(1)} %get-tuple-element.32) | copy-start | bytes 436
  18.9 12.9 %copy-start.11 = (pred[256]{0:T(512)(128)(4,1)}, pred[256]{0:T(512)(128)(4,1)S(1)}, u32[]{:S(2)}) copy-start(pred[256]{0:T(512)(128)(4,1)S(1)} %compare_and_fusion.1) | copy-start | bytes 772
  18.9 0.7 copy-start.5
  19.6 0.7 copy-start.6
  20.5 11.4 %copy-start.13 = (pred[144]{0:T(512)(128)(4,1)}, pred[144]{0:T(512)(128)(4,1)S(1)}, u32[]{:S(2)}) copy-start(pred[144]{0:T(512)(128)(4,1)S(1)} %iota_compare_fusion.5) | copy-start | bytes 436
  77.9 7.3 %copy-start = (bf16[1,3584,128]{2,1,0:T(8,128)(2,1)S(1)}, bf16[1,3584,128]{2,1,0:T(8,128)(2,1)}, u32[]{:S(2)}) copy-start(bf16[1,3584,128]{2,1,0:T(8,128)(2,1)} %param.10) | copy-start | bytes 2752516
  77.9 7.4 %copy-start.1 = (bf16[1,3584,128]{2,1,0:T(8,128)(2,1)S(1)}, bf16[1,3584,128]{2,1,0:T(8,128)(2,1)}, u32[]{:S(2)}) copy-start(bf16[1,3584,128]{2,1,0:T(8,128)(2,1)} %param.11) | copy-start | bytes 2752516
  78.0 20.9 %collective-permute-start = (bf16[288,896]{1,0:T(8,128)(2,1)S(1)}, bf16[288,896]{1,0:T(8,128)(2,1)}, u32[]{:S(2)}, u32[]{:S(2)}) collective-permute-start(bf16[288,896]{1,0:T(8,128)(2,1)S(1)} %get-tuple-element.18.low), channel_id=1, source_target_pairs={{0,64},{64,128},{128,192},{192,256},{256,320},{320,384},{384,448},... | collective-permute-start | bytes 1548296 | tf_op jit(solution)/shard_map/ppermute | solution.py:23
  81.6 17.3 %collective-permute-start.1 = (bf16[288,896]{1,0:T(8,128)(2,1)S(1)}, bf16[288,896]{1,0:T(8,128)(2,1)}, u32[]{:S(2)}, u32[]{:S(2)}) collective-permute-start(bf16[288,896]{1,0:T(8,128)(2,1)S(1)} %get-tuple-element.17.high), channel_id=1, source_target_pairs={{0,960},{64,0},{128,64},{192,128},{256,192},{320,256},{384,320},{4... | collective-permute-start | bytes 1548296 | tf_op jit(solution)/shard_map/ppermute | solution.py:23
  85.2 1.2 copy-start.2
  91.1 0.7 copy-start.4
  91.8 14.1 %collective-permute-start.4 = (bf16[72,1792]{1,0:T(8,128)(2,1)}, bf16[72,1792]{1,0:T(8,128)(2,1)}, u32[]{:S(2)}, u32[]{:S(2)}) collective-permute-start(bf16[72,1792]{1,0:T(8,128)(2,1)} %get-tuple-element.12), channel_id=1, source_target_pairs={{0,64},{64,128},{128,192},{192,256},{256,320},{320,384},{384,448},... | collective-permute-start | bytes 774152 | tf_op jit(solution)/shard_map/ppermute | solution.py:23
  94.6 14.3 %collective-permute-start.2 = (bf16[72,1792]{1,0:T(8,128)(2,1)}, bf16[72,1792]{1,0:T(8,128)(2,1)S(1)}, u32[]{:S(2)}, u32[]{:S(2)}) collective-permute-start(bf16[72,1792]{1,0:T(8,128)(2,1)} %copy-done.4), channel_id=1, source_target_pairs={{0,960},{64,0},{128,64},{192,128},{256,192},{320,256},{384,320},{4... | collective-permute-start | bytes 774152 | tf_op jit(solution)/shard_map/ppermute | solution.py:23
  98.9 1.2 copy-start.3
  107.0 12.2 %collective-permute-start.5 = (bf16[72,3584]{1,0:T(8,128)(2,1)S(1)}, bf16[72,3584]{1,0:T(8,128)(2,1)S(1)}, u32[]{:S(2)}, u32[]{:S(2)}) collective-permute-start(bf16[72,3584]{1,0:T(8,128)(2,1)S(1)} %pad_maximum_fusion.1), channel_id=1, source_target_pairs={{0,64},{64,128},{128,192},{192,256},{256,320},{320,384},{384,448},... | collective-permute-start | bytes 1548296 | tf_op jit(solution)/shard_map/ppermute | solution.py:23
  109.0 11.7 %collective-permute-start.3 = (bf16[72,3584]{1,0:T(8,128)(2,1)S(1)}, bf16[72,3584]{1,0:T(8,128)(2,1)S(1)}, u32[]{:S(2)}, u32[]{:S(2)}) collective-permute-start(bf16[72,3584]{1,0:T(8,128)(2,1)S(1)} %pad_maximum_fusion), channel_id=1, source_target_pairs={{0,960},{64,0},{128,64},{192,128},{256,192},{320,256},{384,320},{4... | collective-permute-start | bytes 1548296 | tf_op jit(solution)/shard_map/ppermute | solution.py:23
  122.1 30.4 %all-to-all-start.1 = ((bf16[4,72,896]{2,1,0:T(8,128)(2,1)}), bf16[4,72,896]{2,1,0:T(8,128)(2,1)S(1)}, u32[]{:S(2)}, u32[]{:S(2)}) async-start(bf16[4,72,896]{2,1,0:T(8,128)(2,1)} %bitcast.8), calls=%async_computation.1 | async-start | bytes 1032192 | tf_op jit(solution)/shard_map/all_to_all | solution.py:219
  129.3 0.7 copy-start.16
  130.0 0.7 copy-start.8
  130.0 0.7 copy-start.10
  130.0 0.7 copy-start.12
  130.0 0.7 copy-start.14
  (1 other events, 0.6 us)

commit v4 on v3

--- a/solution.py
+++ b/solution.py
@@ -35,15 +35,6 @@
     return mask.astype(F32).astype(BF16)
 
 
-def vmem_call(body, out_shape, **kwargs):
-    return pl.pallas_call(
-        body,
-        out_shape=out_shape,
-        compiler_params=pltpu.CompilerParams(vmem_limit_bytes=16 * 2**20),
-        **kwargs,
-    )
-
-
 def spread_kernel(tokens, cotangent, out):
     lanes = out.shape[2]
     rows = [
@@ -52,44 +43,76 @@
     out[...] = jnp.broadcast_to(jnp.concatenate(rows, axis=0)[None], out.shape)
 
 
-def expert_kernel(base, low, high, w_gate, w_up, w_down, *outs):
-    lanes = low.shape[1]
-    middle = low.shape[0]
-    count = base.shape[0]
-    first, second = outs[: len(outs) // 2 + len(outs) % 2], outs[-(len(outs) // 2) :]
-    spots = lax.broadcasted_iota(jnp.int32, (count, middle), 1)
-    gate_pre = up_pre = grad_hid = jnp.zeros((count, w_down.shape[0]), F32)
-    for q in range(QN):
-        cols = slice(q * lanes, (q + 1) * lanes)
-        rows = []
-        for half in range(2):
-            want = base[...] + (half * QN + q) * CAP
-            part = dot(one_hot(spots == want), low[...])
-            part = part + dot(one_hot(spots + middle == want), high[...])
-            rows.append(part.astype(BF16))
-        gate_pre = gate_pre + dot(rows[0], w_gate[cols, :])
-        up_pre = up_pre + dot(rows[0], w_up[cols, :])
-        grad_hid = grad_hid + dot(rows[1], w_down[:, cols], ((1,), (1,)))
+def expert_kernel(zb_last, low_hbm, high_hbm, gate_hbm, up_hbm, down_hbm, *refs):
+    outs, (low, high, w_gate, w_up, w_down, sems) = refs[:-6], refs[-6:]
+    loads = [
+        pltpu.make_async_copy(source, target, sems.at[i])
+        for i, (source, target) in enumerate(
+            (
+                (low_hbm, low),
+                (high_hbm, high),
+                (gate_hbm, w_gate),
+                (up_hbm, w_up),
+                (down_hbm, w_down),
+            )
+        )
+    ]
+    for load in loads:
+        load.start()
+    middle, lanes = low.shape
+    hidden = w_down.shape[0]
+    kept = middle // PIECES
+    padded = (kept + 7) // 8 * 8
+    row = lax.broadcasted_iota(jnp.int32, (PIECES * padded, 1), 0)
+    at = row % padded
+    kind = jnp.where(at < kept // 2, 1 - zb_last[0], zb_last[0])
+    place = at % (kept // 2)
+    want = ((place // CAP * ZB + kind) * PIECES + row // padded) * CAP + place % CAP
+    want = jnp.where(at < kept, want, -1)
+    spots = lax.broadcasted_iota(jnp.int32, (PIECES * padded, middle), 1)
+    pick = one_hot(spots == want)
+    loads[0].wait()
+    from_low = dot(pick, low[...])
+    loads[1].wait()
+    from_high = dot(pick, high[...])
+
+    def rows_of(piece):
+        block = slice(piece * padded, (piece + 1) * padded)
+        return jnp.concatenate([from_low[block], from_high[block]], axis=0).astype(BF16)
+
+    count = 2 * padded
+    pre = jnp.zeros((count, 2 * hidden), F32)
+    grad_hid = jnp.zeros((count, hidden), F32)
+    for load in loads[2:]:
+        load.wait()
+    for q in range(QN):
+        cols = slice(q * lanes, (q + 1) * lanes)
+        pair = jnp.concatenate([w_gate[cols, :], w_up[cols, :]], axis=1)
+        pre = pre + dot(rows_of(q), pair)
+        grad_hid = grad_hid + dot(rows_of(QN + q), w_down[:, cols], ((1,), (1,)))
+    gate_pre, up_pre = pre[:, :hidden], pre[:, hidden:]
     sig = 1.0 / (1.0 + jnp.exp(-gate_pre))
     hid = (gate_pre * sig * up_pre).astype(BF16)
     grad_gate = (grad_hid * up_pre * sig * (1.0 + gate_pre * (1.0 - sig))).astype(BF16)
     grad_up = (grad_hid * gate_pre * sig).astype(BF16)
-    row = lax.broadcasted_iota(jnp.int32, (count, count), 0)
-    col = lax.broadcasted_iota(jnp.int32, (count, count), 1)
-    for kind, refs in enumerate((first, second)):
-        at = col - kind * (count // 2)
-        upper = one_hot((row < count // 2) & (at == row))
-        lower = one_hot((row >= count // 2) & (at == row - count // 2))
-        hid_rows = dot(upper, hid).astype(BF16)
-        gate_rows = dot(lower, grad_gate).astype(BF16)
-        up_rows = dot(lower, grad_up).astype(BF16)
-        for q in range(QN):
-            cols = slice(q * lanes, (q + 1) * lanes)
-            term = dot(hid_rows, w_down[:, cols])
-            term = term + dot(gate_rows, w_gate[cols, :], ((1,), (1,)))
-            term = term + dot(up_rows, w_up[cols, :], ((1,), (1,)))
-            each = QN // len(refs)
-            refs[q // each][:, q % each * lanes : (q % each + 1) * lanes] = term.astype(BF16)
+    grads = jnp.concatenate([grad_gate, grad_up], axis=1)
+    group = 2 * ZA * CAP
+    back = lax.broadcasted_iota(jnp.int32, (2 * group, 1), 0)
+    za = back // CAP % ZA
+    source = za // 2 * padded + back // group * (kept // 2) + za % 2 * CAP + back % CAP
+    second = back // (ZA * CAP) % 2
+    taken = lax.broadcasted_iota(jnp.int32, (2 * group, count), 1)
+    hid_rows = dot(one_hot(taken == jnp.where(second == 0, source, -1)), hid).astype(BF16)
+    grad_rows = dot(one_hot(taken == jnp.where(second == 1, source, -1)), grads).astype(BF16)
+    first, last = outs[: len(outs) // 2 + len(outs) % 2], outs[-(len(outs) // 2) :]
+    for q in range(QN):
+        cols = slice(q * lanes, (q + 1) * lanes)
+        pair = jnp.concatenate([w_gate[cols, :], w_up[cols, :]], axis=1)
+        term = dot(hid_rows, w_down[:, cols]) + dot(grad_rows, pair, ((1,), (1,)))
+        for kind, parts in enumerate((first, last)):
+            each = QN // len(parts)
+            target = slice(q % each * lanes, (q % each + 1) * lanes)
+            parts[q // each][:, target] = term[kind * group : (kind + 1) * group].astype(BF16)
 
 
 def pack_kernel(source, here, above, below, out):
@@ -169,12 +192,6 @@
     zb = lax.axis_index("zb").astype(jnp.int32)
     zd = lax.axis_index("zd").astype(jnp.int32)
     group = ZA * 2 * CAP
-    index = jnp.arange(group, dtype=jnp.int32)[:, None]
-
-    def base_of(last):
-        at = jnp.where(index < group // 2, 1 - last, last)
-        return (index // CAP % ZA * ZB + at) * PACK + index % CAP
-
     same = lax.all_gather(packed, ("za", "zb"), axis=0, tiled=True)
     middle = same.shape[0] // 2
     from_below = shift_z(same[:middle], 1)
@@ -182,13 +199,21 @@
 
     def expert_terms(last, lower, upper, splits):
         width_of = [width // n for n in splits for _ in range(n)]
-        return vmem_call(
+        weights = (w_gate, w_up, w_down)
+        hbm = pl.BlockSpec(memory_space=pl.ANY)
+        return pl.pallas_call(
             expert_kernel,
-            [jax.ShapeDtypeStruct((group, w), BF16) for w in width_of],
+            out_shape=[jax.ShapeDtypeStruct((group, w), BF16) for w in width_of],
+            in_specs=[pl.BlockSpec(memory_space=pltpu.SMEM)] + [hbm] * 5,
+            scratch_shapes=[pltpu.VMEM(v.shape, BF16) for v in (lower, upper) + weights]
+            + [pltpu.SemaphoreType.DMA((5,))],
+            compiler_params=pltpu.CompilerParams(vmem_limit_bytes=62 * 2**20),
             cost_estimate=pl.CostEstimate(
-                flops=36 * group * width * w_down.shape[0], bytes_accessed=12 * width * w_down.shape[0], transcendentals=0
+                flops=36 * group * width * w_down.shape[0],
+                bytes_accessed=12 * width * w_down.shape[0],
+                transcendentals=0,
             ),
-        )(base_of(last), lower, upper, w_gate, w_up, w_down)
+        )(last[None], lower, upper, *weights)
 
     far_left, far_right, terms_here = expert_terms(zb, same[:middle], same[middle:], (2, 1))
 
@@ -213,7 +238,11 @@
     )
     row = jnp.arange(ZA * PACK, dtype=jnp.int32)[:, None]
     source = (row // CAP % QN) * group + (row // (QN * CAP) % 2 * ZA + row // PACK) * CAP
-    outgoing = vmem_call(pack_kernel, jax.ShapeDtypeStruct((ZA * PACK, lanes), BF16))(
+    outgoing = pl.pallas_call(
+        pack_kernel,
+        out_shape=jax.ShapeDtypeStruct((ZA * PACK, lanes), BF16),
+        compiler_params=pltpu.CompilerParams(vmem_limit_bytes=16 * 2**20),
+    )(
         source + row % CAP, terms_here, shift_z(low, -1), shift_z(high, 1)
     ).reshape(ZA, PACK, lanes)
     arrived = lax.all_to_all(outgoing, "za", 0, 0, tiled=True)

time: 181 us -> 177 us (0.978)
  local copies, waits for them, and re-layouts: 6.4 us -> 2.71 us
    unnamed x34 -> x14, local copies, waits for them, and re-layouts: 6.17 us -> 1.46 us
where the time goes in v4:
time: 177 us; the launch traced here: 176 us
  blocking collectives  71.1 us (40%)
  starting transfers between devices  44.8 us (25%)
  waiting for transfers between devices  39.8 us (22%)
  Pallas kernels  14.4 us (8%)
  local copies, waits for them, and re-layouts  2.71 us (2%)
    all_gather x1, blocking collectives, local(): same = lax.all_gather(packed, ('za', 'zb'), axis=0, tiled=True)  43.8 us
    all_to_all x1, blocking collectives, local(): mine = lax.all_to_all(dense, PLANE, 0, 0, tiled=True)  23.3 us
    all_to_all x1, waiting for transfers between devices, local(): arrived = lax.all_to_all(outgoing, 'za', 0, 0, tiled=True)  22.2 us
    ppermute x6, starting transfers between devices, shift_z(): return lax.ppermute(values, ZAXES, [(i, (i + step) % n) for i in range(n)])  21.4 us
    all_to_all x1, starting transfers between devices, local(): lax.all_to_all(spread, PLANE, 0, 0, tiled=True)  16.6 us
    all_to_all x1, waiting for transfers between devices, local(): lax.all_to_all(spread, PLANE, 0, 0, tiled=True)  11.2 us
    pallas_call x2, Pallas kernels, expert_terms(): pl.pallas_call(expert_kernel, out_shape=[jax.ShapeDtypeStruct((group, w),...  9.78 us
    all_to_all x1, starting transfers between devices, local(): arrived = lax.all_to_all(outgoing, 'za', 0, 0, tiled=True)  6.7 us
  transfers between devices with their start and end apart: 8, of which 4 were waited for; matrix products, arithmetic and copies ran while one was open for 1% of the time, Pallas kernels for 6%

profile of v4, /device:TPU:8, one launch (start us, length us, event | category | flops | bytes accessed | tf_op | source)
XLA Modules:
  0.0 176.4 jit_solution(1562486515349448963)
XLA Ops:
  0.6 1.6 shard_map.94
  2.2 16.6 %all-to-all-start = ((bf16[32,8,896]{2,1,0:T(8,128)(2,1)}), bf16[32,8,896]{2,1,0:T(8,128)(2,1)S(1)}, u32[]{:S(2)}, u32[]{:S(2)}) async-start(bf16[32,8,896]{2,1,0:T(8,128)(2,1)} %shard_map.94), calls=%async_computation | async-start | bytes 917504 | tf_op jit(solution)/shard_map/all_to_all | solution.py:161
  18.9 0.7 copy-done.5
  19.6 0.7 copy-done.6
  20.6 11.2 %all-to-all-done = bf16[32,8,896]{2,1,0:T(8,128)(2,1)S(1)} async-done(((bf16[32,8,896]{2,1,0:T(8,128)(2,1)}), bf16[32,8,896]{2,1,0:T(8,128)(2,1)S(1)}, u32[]{:S(2)}, u32[]{:S(2)}) %all-to-all-start) | async-done | bytes 458784 | tf_op jit(solution)/shard_map/all_to_all | solution.py:161
  32.2 2.0 %all-gather = bf16[144,896]{1,0:T(8,128)(2,1)S(1)} all-gather(bf16[72,896]{1,0:T(8,128)(2,1)S(1)} %slice.82), channel_id=2, replica_groups=mesh['za'=4,'zb'=2,'zd'=2,'x'=4,'y'=8,'c'=2] {'c'}, dimensions={0}, use_global_device_ids=true | all-gather | bytes 387072 | tf_op jit(solution)/shard_map/all_gather | solution.py:27
  34.2 43.8 %all_gather.15 = bf16[576,896]{1,0:T(8,128)(2,1)S(1)} all-gather(bf16[72,896]{1,0:T(8,128)(2,1)S(1)} %fusion.26), channel_id=1, replica_groups=mesh['za'=4,'zb'=2,'zd'=2,'x'=4,'y'=8,'c'=2] {'za','zb'}, dimensions={0}, use_global_device_ids=true | all-gather | bytes 1161216 | tf_op jit(solution)/shard_map/all_gather | solution.py:195
  78.2 3.0 %collective-permute-start = (bf16[288,896]{1,0:T(8,128)(2,1)S(1)}, bf16[288,896]{1,0:T(8,128)(2,1)}, u32[]{:S(2)}, u32[]{:S(2)}) collective-permute-start(bf16[288,896]{1,0:T(8,128)(2,1)S(1)} %get-tuple-element.18.low_hbm), channel_id=1, source_target_pairs={{0,64},{64,128},{128,192},{192,256},{256,320},{320,384},{384,448},... | collective-permute-start | bytes 1548296 | tf_op jit(solution)/shard_map/ppermute | solution.py:23
  81.2 4.0 %collective-permute-start.1 = (bf16[288,896]{1,0:T(8,128)(2,1)S(1)}, bf16[288,896]{1,0:T(8,128)(2,1)}, u32[]{:S(2)}, u32[]{:S(2)}) collective-permute-start(bf16[288,896]{1,0:T(8,128)(2,1)S(1)} %get-tuple-element.17.high_hbm), channel_id=1, source_target_pairs={{0,960},{64,0},{128,64},{192,128},{256,192},{320,256},{384,320},{4... | collective-permute-start | bytes 1548296 | tf_op jit(solution)/shard_map/ppermute | solution.py:23
  85.3 4.8 %shard_map.95 = (bf16[72,1792]{1,0:T(8,128)(2,1)}, bf16[72,1792]{1,0:T(8,128)(2,1)}, bf16[72,3584]{1,0:T(8,128)(2,1)}) custom-call(s32[1]{0:T(128)} %bitcast.4.zb_last, bf16[288,896]{1,0:T(8,128)(2,1)} %copy-done.4, bf16[288,896]{1,0:T(8,128)(2,1)} %copy-done.3, bf16[3584,128]{1,0:T(8,128)(2,1)} %bitcast.33, bf16[3584,128]{1,0:T(8,128)(2,1)} %bitcast.35, ...), custom_call_target="tpu_custom_call" | custom-call | flops 1189085184 | bytes 5505024 | tf_op jit(solution)/shard_map/pallas_call | solution.py:204
  90.1 2.9 %collective-permute-start.4 = (bf16[72,1792]{1,0:T(8,128)(2,1)}, bf16[72,1792]{1,0:T(8,128)(2,1)S(1)}, u32[]{:S(2)}, u32[]{:S(2)}) collective-permute-start(bf16[72,1792]{1,0:T(8,128)(2,1)} %get-tuple-element.12), channel_id=1, source_target_pairs={{0,64},{64,128},{128,192},{192,256},{256,320},{320,384},{384,448},... | collective-permute-start | bytes 774152 | tf_op jit(solution)/shard_map/ppermute | solution.py:23
  93.0 4.2 %collective-permute-start.2 = (bf16[72,1792]{1,0:T(8,128)(2,1)}, bf16[72,1792]{1,0:T(8,128)(2,1)S(1)}, u32[]{:S(2)}, u32[]{:S(2)}) collective-permute-start(bf16[72,1792]{1,0:T(8,128)(2,1)} %get-tuple-element.10), channel_id=1, source_target_pairs={{0,960},{64,0},{128,64},{192,128},{256,192},{320,256},{384,320},{4... | collective-permute-start | bytes 774152 | tf_op jit(solution)/shard_map/ppermute | solution.py:23
  97.2 4.9 %shard_map.96 = (bf16[72,3584]{1,0:T(8,128)(2,1)}, bf16[72,3584]{1,0:T(8,128)(2,1)}) custom-call(s32[1]{0:T(128)} %bitcast.9.zb_last, bf16[288,896]{1,0:T(8,128)(2,1)} %collective-permute-done.low_hbm, bf16[288,896]{1,0:T(8,128)(2,1)} %collective-permute-done.1.high_hbm, bf16[3584,128]{1,0:T(8,128)(2,1)} %bitcast.34, bf16[3584,128]{1,0:T(8,128)(2,1)} %bitcast.36, ...), custom_call_target="tpu_custom_call" | custom-call | flops 1189085184 | bytes 5505024 | tf_op jit(solution)/shard_map/pallas_call | solution.py:204
  102.2 1.0 slice.69
  103.5 2.2 %collective-permute-start.5 = (bf16[72,3584]{1,0:T(8,128)(2,1)S(1)}, bf16[72,3584]{1,0:T(8,128)(2,1)S(1)}, u32[]{:S(2)}, u32[]{:S(2)}) collective-permute-start(bf16[72,3584]{1,0:T(8,128)(2,1)S(1)} %pad_maximum_fusion.1), channel_id=1, source_target_pairs={{0,64},{64,128},{128,192},{192,256},{256,320},{320,384},{384,448},... | collective-permute-start | bytes 1548296 | tf_op jit(solution)/shard_map/ppermute | solution.py:23
  105.9 5.1 %collective-permute-start.3 = (bf16[72,3584]{1,0:T(8,128)(2,1)S(1)}, bf16[72,3584]{1,0:T(8,128)(2,1)S(1)}, u32[]{:S(2)}, u32[]{:S(2)}) collective-permute-start(bf16[72,3584]{1,0:T(8,128)(2,1)S(1)} %pad_maximum_fusion), channel_id=1, source_target_pairs={{0,960},{64,0},{128,64},{192,128},{256,192},{320,256},{384,320},{4... | collective-permute-start | bytes 1548296 | tf_op jit(solution)/shard_map/ppermute | solution.py:23
  111.2 4.6 %collective-permute-done.5.below = bf16[72,3584]{1,0:T(8,128)(2,1)S(1)} collective-permute-done((bf16[72,3584]{1,0:T(8,128)(2,1)S(1)}, bf16[72,3584]{1,0:T(8,128)(2,1)S(1)}, u32[]{:S(2)}, u32[]{:S(2)}) %collective-permute-start.5) | collective-permute-done | bytes 516128 | tf_op jit(solution)/shard_map/ppermute | solution.py:23
  115.8 1.8 %collective-permute-done.3.above = bf16[72,3584]{1,0:T(8,128)(2,1)S(1)} collective-permute-done((bf16[72,3584]{1,0:T(8,128)(2,1)S(1)}, bf16[72,3584]{1,0:T(8,128)(2,1)S(1)}, u32[]{:S(2)}, u32[]{:S(2)}) %collective-permute-start.3) | collective-permute-done | bytes 516128 | tf_op jit(solution)/shard_map/ppermute | solution.py:23
  117.6 1.3 shard_map.97
  118.9 6.7 %all-to-all-start.1 = ((bf16[4,72,896]{2,1,0:T(8,128)(2,1)}), bf16[4,72,896]{2,1,0:T(8,128)(2,1)S(1)}, u32[]{:S(2)}, u32[]{:S(2)}) async-start(bf16[4,72,896]{2,1,0:T(8,128)(2,1)} %bitcast.10), calls=%async_computation.1 | async-start | bytes 1032192 | tf_op jit(solution)/shard_map/all_to_all | solution.py:248
  126.0 22.2 %all-to-all-done.1 = bf16[4,72,896]{2,1,0:T(8,128)(2,1)S(1)} async-done(((bf16[4,72,896]{2,1,0:T(8,128)(2,1)}), bf16[4,72,896]{2,1,0:T(8,128)(2,1)S(1)}, u32[]{:S(2)}, u32[]{:S(2)}) %all-to-all-start.1) | async-done | bytes 516128 | tf_op jit(solution)/shard_map/all_to_all | solution.py:248
  148.8 2.0 %all_gather.16 = bf16[2,72,1024]{2,1,0:T(8,128)(2,1)S(1)} all-gather(bf16[1,72,1024]{2,1,0:T(8,128)(2,1)S(1)} %pad_maximum_fusion.2), channel_id=1, replica_groups=mesh['za'=4,'zb'=2,'zd'=2,'x'=4,'y'=8,'c'=2] {'c'}, dimensions={0}, use_global_device_ids=true | all-gather | bytes 442368 | tf_op jit(solution)/shard_map/all_gather | solution.py:27
  151.3 23.3 %all_to_all.15.mine = bf16[32,8,1024]{2,1,0:T(8,128)(2,1)} all-to-all(bf16[32,8,1024]{2,1,0:T(8,128)(2,1)S(1)} %fusion), channel_id=1, replica_groups=mesh['za'=4,'zb'=2,'zd'=2,'x'=4,'y'=8,'c'=2] {'x','y'}, dimensions={0} | all-to-all | bytes 1048576 | tf_op jit(solution)/shard_map/all_to_all | solution.py:266
  174.6 1.7 shard_map.98
  (56 shorter events, 3.0 us)
Async XLA Ops:
  2.2 29.6 %all-to-all-start = ((bf16[32,8,896]{2,1,0:T(8,128)(2,1)}), bf16[32,8,896]{2,1,0:T(8,128)(2,1)S(1)}, u32[]{:S(2)}, u32[]{:S(2)}) async-start(bf16[32,8,896]{2,1,0:T(8,128)(2,1)} %shard_map.94), calls=%async_computation | async-start | bytes 917504 | tf_op jit(solution)/shard_map/all_to_all | solution.py:161
  18.9 0.7 copy-start.5
  19.6 0.7 copy-start.6
  78.2 7.1 %copy-start.3 = (bf16[288,896]{1,0:T(8,128)(2,1)}, bf16[288,896]{1,0:T(8,128)(2,1)S(1)}, u32[]{:S(2)}) copy-start(bf16[288,896]{1,0:T(8,128)(2,1)S(1)} %get-tuple-element.17.high_hbm) | copy-start | bytes 1548292
  78.2 7.1 %copy-start.4 = (bf16[288,896]{1,0:T(8,128)(2,1)}, bf16[288,896]{1,0:T(8,128)(2,1)S(1)}, u32[]{:S(2)}) copy-start(bf16[288,896]{1,0:T(8,128)(2,1)S(1)} %get-tuple-element.18.low_hbm) | copy-start | bytes 1548292
  78.2 19.0 %collective-permute-start = (bf16[288,896]{1,0:T(8,128)(2,1)S(1)}, bf16[288,896]{1,0:T(8,128)(2,1)}, u32[]{:S(2)}, u32[]{:S(2)}) collective-permute-start(bf16[288,896]{1,0:T(8,128)(2,1)S(1)} %get-tuple-element.18.low_hbm), channel_id=1, source_target_pairs={{0,64},{64,128},{128,192},{192,256},{256,320},{320,384},{384,448},... | collective-permute-start | bytes 1548296 | tf_op jit(solution)/shard_map/ppermute | solution.py:23
  81.2 16.0 %collective-permute-start.1 = (bf16[288,896]{1,0:T(8,128)(2,1)S(1)}, bf16[288,896]{1,0:T(8,128)(2,1)}, u32[]{:S(2)}, u32[]{:S(2)}) collective-permute-start(bf16[288,896]{1,0:T(8,128)(2,1)S(1)} %get-tuple-element.17.high_hbm), channel_id=1, source_target_pairs={{0,960},{64,0},{128,64},{192,128},{256,192},{320,256},{384,320},{4... | collective-permute-start | bytes 1548296 | tf_op jit(solution)/shard_map/ppermute | solution.py:23
  90.1 13.1 %collective-permute-start.4 = (bf16[72,1792]{1,0:T(8,128)(2,1)}, bf16[72,1792]{1,0:T(8,128)(2,1)S(1)}, u32[]{:S(2)}, u32[]{:S(2)}) collective-permute-start(bf16[72,1792]{1,0:T(8,128)(2,1)} %get-tuple-element.12), channel_id=1, source_target_pairs={{0,64},{64,128},{128,192},{192,256},{256,320},{320,384},{384,448},... | collective-permute-start | bytes 774152 | tf_op jit(solution)/shard_map/ppermute | solution.py:23
  93.0 12.7 %collective-permute-start.2 = (bf16[72,1792]{1,0:T(8,128)(2,1)}, bf16[72,1792]{1,0:T(8,128)(2,1)S(1)}, u32[]{:S(2)}, u32[]{:S(2)}) collective-permute-start(bf16[72,1792]{1,0:T(8,128)(2,1)} %get-tuple-element.10), channel_id=1, source_target_pairs={{0,960},{64,0},{128,64},{192,128},{256,192},{320,256},{384,320},{4... | collective-permute-start | bytes 774152 | tf_op jit(solution)/shard_map/ppermute | solution.py:23
  102.2 1.2 copy-start.2
  103.4 2.3 %copy-start.1 = (bf16[72,3584]{1,0:T(8,128)(2,1)S(1)}, bf16[72,3584]{1,0:T(8,128)(2,1)}, u32[]{:S(2)}) copy-start(bf16[72,3584]{1,0:T(8,128)(2,1)} %get-tuple-element.9) | copy-start | bytes 1548292
  103.5 12.3 %collective-permute-start.5 = (bf16[72,3584]{1,0:T(8,128)(2,1)S(1)}, bf16[72,3584]{1,0:T(8,128)(2,1)S(1)}, u32[]{:S(2)}, u32[]{:S(2)}) collective-permute-start(bf16[72,3584]{1,0:T(8,128)(2,1)S(1)} %pad_maximum_fusion.1), channel_id=1, source_target_pairs={{0,64},{64,128},{128,192},{192,256},{256,320},{320,384},{384,448},... | collective-permute-start | bytes 1548296 | tf_op jit(solution)/shard_map/ppermute | solution.py:23
  105.8 11.7 %copy-start = (bf16[72,3584]{1,0:T(8,128)(2,1)S(1)}, bf16[72,3584]{1,0:T(8,128)(2,1)}, u32[]{:S(2)}) copy-start(bf16[72,3584]{1,0:T(8,128)(2,1)} %get-tuple-element.8.here) | copy-start | bytes 1548292
  105.9 11.7 %collective-permute-start.3 = (bf16[72,3584]{1,0:T(8,128)(2,1)S(1)}, bf16[72,3584]{1,0:T(8,128)(2,1)S(1)}, u32[]{:S(2)}, u32[]{:S(2)}) collective-permute-start(bf16[72,3584]{1,0:T(8,128)(2,1)S(1)} %pad_maximum_fusion), channel_id=1, source_target_pairs={{0,960},{64,0},{128,64},{192,128},{256,192},{320,256},{384,320},{4... | collective-permute-start | bytes 1548296 | tf_op jit(solution)/shard_map/ppermute | solution.py:23
  118.9 29.2 %all-to-all-start.1 = ((bf16[4,72,896]{2,1,0:T(8,128)(2,1)}), bf16[4,72,896]{2,1,0:T(8,128)(2,1)S(1)}, u32[]{:S(2)}, u32[]{:S(2)}) async-start(bf16[4,72,896]{2,1,0:T(8,128)(2,1)} %bitcast.10), calls=%async_computation.1 | async-start | bytes 1032192 | tf_op jit(solution)/shard_map/all_to_all | solution.py:248

commit v5 on v4

--- a/solution.py
+++ b/solution.py
@@ -43,22 +43,7 @@
     out[...] = jnp.broadcast_to(jnp.concatenate(rows, axis=0)[None], out.shape)
 
 
-def expert_kernel(zb_last, low_hbm, high_hbm, gate_hbm, up_hbm, down_hbm, *refs):
-    outs, (low, high, w_gate, w_up, w_down, sems) = refs[:-6], refs[-6:]
-    loads = [
-        pltpu.make_async_copy(source, target, sems.at[i])
-        for i, (source, target) in enumerate(
-            (
-                (low_hbm, low),
-                (high_hbm, high),
-                (gate_hbm, w_gate),
-                (up_hbm, w_up),
-                (down_hbm, w_down),
-            )
-        )
-    ]
-    for load in loads:
-        load.start()
+def expert_kernel(zb_last, low, high, w_gate, w_up, w_down, *outs):
     middle, lanes = low.shape
     hidden = w_down.shape[0]
     kept = middle // PIECES
@@ -71,9 +56,7 @@
     want = jnp.where(at < kept, want, -1)
     spots = lax.broadcasted_iota(jnp.int32, (PIECES * padded, middle), 1)
     pick = one_hot(spots == want)
-    loads[0].wait()
     from_low = dot(pick, low[...])
-    loads[1].wait()
     from_high = dot(pick, high[...])
 
     def rows_of(piece):
@@ -83,8 +66,6 @@
     count = 2 * padded
     pre = jnp.zeros((count, 2 * hidden), F32)
     grad_hid = jnp.zeros((count, hidden), F32)
-    for load in loads[2:]:
-        load.wait()
     for q in range(QN):
         cols = slice(q * lanes, (q + 1) * lanes)
         pair = jnp.concatenate([w_gate[cols, :], w_up[cols, :]], axis=1)
@@ -200,14 +181,11 @@
     def expert_terms(last, lower, upper, splits):
         width_of = [width // n for n in splits for _ in range(n)]
         weights = (w_gate, w_up, w_down)
-        hbm = pl.BlockSpec(memory_space=pl.ANY)
         return pl.pallas_call(
             expert_kernel,
             out_shape=[jax.ShapeDtypeStruct((group, w), BF16) for w in width_of],
-            in_specs=[pl.BlockSpec(memory_space=pltpu.SMEM)] + [hbm] * 5,
-            scratch_shapes=[pltpu.VMEM(v.shape, BF16) for v in (lower, upper) + weights]
-            + [pltpu.SemaphoreType.DMA((5,))],
-            compiler_params=pltpu.CompilerParams(vmem_limit_bytes=62 * 2**20),
+            in_specs=[pl.BlockSpec(memory_space=pltpu.SMEM)] + [pl.BlockSpec()] * 5,
+            compiler_params=pltpu.CompilerParams(vmem_limit_bytes=16 * 2**20),
             cost_estimate=pl.CostEstimate(
                 flops=36 * group * width * w_down.shape[0],
                 bytes_accessed=12 * width * w_down.shape[0],
@@ -222,19 +200,15 @@
     terms_below, terms_above = expert_terms(
         jnp.where(zd == 1, 1 - zb, zb), from_below, from_above, (1, 1)
     )
-    low = jnp.concatenate(
-        [
-            (terms_below[:, :half_width].astype(F32) + back_left.astype(F32)).astype(BF16),
-            terms_below[:, half_width:],
-        ],
-        axis=1,
-    )
-    high = jnp.concatenate(
-        [
-            terms_above[:, :half_width],
-            (terms_above[:, half_width:].astype(F32) + back_right.astype(F32)).astype(BF16),
-        ],
-        axis=1,
+    low = lax.dynamic_update_slice(
+        terms_below,
+        (terms_below[:, :half_width].astype(F32) + back_left.astype(F32)).astype(BF16),
+        (0, 0),
+    )
+    high = lax.dynamic_update_slice(
+        terms_above,
+        (terms_above[:, half_width:].astype(F32) + back_right.astype(F32)).astype(BF16),
+        (0, half_width),
     )
     row = jnp.arange(ZA * PACK, dtype=jnp.int32)[:, None]
     source = (row // CAP % QN) * group + (row // (QN * CAP) % 2 * ZA + row // PACK) * CAP

time: 177 us -> 178 us (level)
  local copies, waits for them, and re-layouts: 2.71 us -> 6.37 us
  Pallas kernels: 14.4 us -> 12.1 us
    unnamed x14 -> x34, local copies, waits for them, and re-layouts: 1.46 us -> 6.18 us
    pallas_call x2, Pallas kernels: 9.78 us -> 7.53 us  [expert_terms(): pl.pallas_call(expert_kernel, out_shape=[jax.ShapeDtypeStruct((group, w),...]
  transfers between devices with their start and end apart: 8 -> 8, of which waited for: 4 -> 4; matrix products, arithmetic and copies ran while one was open for 1% -> 1% of each run, Pallas kernels for 6% -> 4%
where the time goes in v5:
time: 178 us; the launch traced here: 177 us
  blocking collectives  70.6 us (40%)
  starting transfers between devices  45.1 us (25%)
  waiting for transfers between devices  38.7 us (22%)
  Pallas kernels  12.1 us (7%)
  local copies, waits for them, and re-layouts  6.37 us (4%)
  other arithmetic  2.29 us (1%)
    all_gather x1, blocking collectives, local(): same = lax.all_gather(packed, ('za', 'zb'), axis=0, tiled=True)  43.6 us
    all_to_all x1, blocking collectives, local(): mine = lax.all_to_all(dense, PLANE, 0, 0, tiled=True)  22.9 us
    all_to_all x1, waiting for transfers between devices, local(): arrived = lax.all_to_all(outgoing, 'za', 0, 0, tiled=True)  21.6 us
    ppermute x6, starting transfers between devices, shift_z(): return lax.ppermute(values, ZAXES, [(i, (i + step) % n) for i in range(n)])  21.3 us
    all_to_all x1, starting transfers between devices, local(): lax.all_to_all(spread, PLANE, 0, 0, tiled=True)  16.6 us
    all_to_all x1, waiting for transfers between devices, local(): lax.all_to_all(spread, PLANE, 0, 0, tiled=True)  10.7 us
    pallas_call x2, Pallas kernels, expert_terms(): pl.pallas_call(expert_kernel, out_shape=[jax.ShapeDtypeStruct((group, w),...  7.53 us
    all_to_all x1, starting transfers between devices, local(): arrived = lax.all_to_all(outgoing, 'za', 0, 0, tiled=True)  7.2 us
  transfers between devices with their start and end apart: 8, of which 4 were waited for; matrix products, arithmetic and copies ran while one was open for 1% of the time, Pallas kernels for 4%

profile of v5, /device:TPU:8, one launch (start us, length us, event | category | flops | bytes accessed | tf_op | source)
XLA Modules:
  0.0 177.5 jit_solution(10706368566513596053)
XLA Ops:
  0.6 1.5 shard_map.94
  2.2 16.6 %all-to-all-start = ((bf16[32,8,896]{2,1,0:T(8,128)(2,1)}), bf16[32,8,896]{2,1,0:T(8,128)(2,1)S(1)}, u32[]{:S(2)}, u32[]{:S(2)}) async-start(bf16[32,8,896]{2,1,0:T(8,128)(2,1)} %shard_map.94), calls=%async_computation | async-start | bytes 917504 | tf_op jit(solution)/shard_map/all_to_all | solution.py:142
  21.2 10.7 %all-to-all-done = bf16[32,8,896]{2,1,0:T(8,128)(2,1)S(1)} async-done(((bf16[32,8,896]{2,1,0:T(8,128)(2,1)}), bf16[32,8,896]{2,1,0:T(8,128)(2,1)S(1)}, u32[]{:S(2)}, u32[]{:S(2)}) %all-to-all-start) | async-done | bytes 458784 | tf_op jit(solution)/shard_map/all_to_all | solution.py:142
  32.2 2.0 %all-gather = bf16[144,896]{1,0:T(8,128)(2,1)S(1)} all-gather(bf16[72,896]{1,0:T(8,128)(2,1)S(1)} %slice.74), channel_id=2, replica_groups=mesh['za'=4,'zb'=2,'zd'=2,'x'=4,'y'=8,'c'=2] {'c'}, dimensions={0}, use_global_device_ids=true | all-gather | bytes 387072 | tf_op jit(solution)/shard_map/all_gather | solution.py:27
  34.3 43.6 %all_gather.15 = bf16[576,896]{1,0:T(8,128)(2,1)S(1)} all-gather(bf16[72,896]{1,0:T(8,128)(2,1)S(1)} %fusion.28), channel_id=1, replica_groups=mesh['za'=4,'zb'=2,'zd'=2,'x'=4,'y'=8,'c'=2] {'za','zb'}, dimensions={0}, use_global_device_ids=true | all-gather | bytes 1161216 | tf_op jit(solution)/shard_map/all_gather | solution.py:176
  78.0 3.6 %collective-permute-start = (bf16[288,896]{1,0:T(8,128)(2,1)S(1)}, bf16[288,896]{1,0:T(8,128)(2,1)}, u32[]{:S(2)}, u32[]{:S(2)}) collective-permute-start(bf16[288,896]{1,0:T(8,128)(2,1)S(1)} %get-tuple-element.18.low), channel_id=1, source_target_pairs={{0,64},{64,128},{128,192},{192,256},{256,320},{320,384},{384,448},... | collective-permute-start | bytes 1548296 | tf_op jit(solution)/shard_map/ppermute | solution.py:23
  81.6 3.6 %collective-permute-start.1 = (bf16[288,896]{1,0:T(8,128)(2,1)S(1)}, bf16[288,896]{1,0:T(8,128)(2,1)}, u32[]{:S(2)}, u32[]{:S(2)}) collective-permute-start(bf16[288,896]{1,0:T(8,128)(2,1)S(1)} %get-tuple-element.17.high), channel_id=1, source_target_pairs={{0,960},{64,0},{128,64},{192,128},{256,192},{320,256},{384,320},{4... | collective-permute-start | bytes 1548296 | tf_op jit(solution)/shard_map/ppermute | solution.py:23
  85.2 1.2 copy-done.2
  86.4 3.5 %shard_map.95 = (bf16[72,1792]{1,0:T(8,128)(2,1)S(1)}, bf16[72,1792]{1,0:T(8,128)(2,1)}, bf16[72,3584]{1,0:T(8,128)(2,1)S(1)}) custom-call(s32[1]{0:T(128)} %bitcast.4.zb_last, bf16[288,896]{1,0:T(8,128)(2,1)S(1)} %get-tuple-element.18.low, bf16[288,896]{1,0:T(8,128)(2,1)S(1)} %get-tuple-element.17.high, bf16[3584,128]{1,0:T(8,128)(2,1)S(1)} %bitcast.24, ...), custom_call_target="tpu_custom_call" | custom-call | flops 1189085184 | bytes 5505024 | tf_op jit(solution)/shard_map/pallas_call | solution.py:184
  90.6 2.8 %collective-permute-start.4 = (bf16[72,1792]{1,0:T(8,128)(2,1)}, bf16[72,1792]{1,0:T(8,128)(2,1)}, u32[]{:S(2)}, u32[]{:S(2)}) collective-permute-start(bf16[72,1792]{1,0:T(8,128)(2,1)} %get-tuple-element.12), channel_id=1, source_target_pairs={{0,64},{64,128},{128,192},{192,256},{256,320},{320,384},{384,448},... | collective-permute-start | bytes 774152 | tf_op jit(solution)/shard_map/ppermute | solution.py:23
  93.4 4.2 %collective-permute-start.2 = (bf16[72,1792]{1,0:T(8,128)(2,1)}, bf16[72,1792]{1,0:T(8,128)(2,1)S(1)}, u32[]{:S(2)}, u32[]{:S(2)}) collective-permute-start(bf16[72,1792]{1,0:T(8,128)(2,1)} %copy-done.4), channel_id=1, source_target_pairs={{0,960},{64,0},{128,64},{192,128},{256,192},{320,256},{384,320},{4... | collective-permute-start | bytes 774152 | tf_op jit(solution)/shard_map/ppermute | solution.py:23
  97.7 1.2 copy-done.3
  98.9 4.0 %shard_map.96 = (bf16[72,3584]{1,0:T(8,128)(2,1)S(1)}, bf16[72,3584]{1,0:T(8,128)(2,1)S(1)}) custom-call(s32[1]{0:T(128)} %bitcast.9.zb_last, bf16[288,896]{1,0:T(8,128)(2,1)} %collective-permute-done.low, bf16[288,896]{1,0:T(8,128)(2,1)} %collective-permute-done.1.high, bf16[3584,128]{1,0:T(8,128)(2,1)S(1)} %bitcast.25, bf16[3584,128]{1,0:T(8,128)(2,1)S(1)} %bitcast.27, ...), custom_call_target="tpu_custom_call" | custom-call | flops 1189085184 | bytes 5505024 | tf_op jit(solution)/shard_map/pallas_call | solution.py:184
  102.9 1.1 fusion.8
  104.0 1.9 %collective-permute-start.5 = (bf16[72,3584]{1,0:T(8,128)(2,1)S(1)}, bf16[72,3584]{1,0:T(8,128)(2,1)S(1)}, u32[]{:S(2)}, u32[]{:S(2)}) collective-permute-start(bf16[72,3584]{1,0:T(8,128)(2,1)S(1)} %fusion.8), channel_id=1, source_target_pairs={{0,64},{64,128},{128,192},{192,256},{256,320},{320,384},{384,448},... | collective-permute-start | bytes 1548296 | tf_op jit(solution)/shard_map/ppermute | solution.py:23
  106.0 5.1 %collective-permute-start.3 = (bf16[72,3584]{1,0:T(8,128)(2,1)S(1)}, bf16[72,3584]{1,0:T(8,128)(2,1)S(1)}, u32[]{:S(2)}, u32[]{:S(2)}) collective-permute-start(bf16[72,3584]{1,0:T(8,128)(2,1)S(1)} %fusion.7), channel_id=1, source_target_pairs={{0,960},{64,0},{128,64},{192,128},{256,192},{320,256},{384,320},{4... | collective-permute-start | bytes 1548296 | tf_op jit(solution)/shard_map/ppermute | solution.py:23
  111.4 4.8 %collective-permute-done.5.below = bf16[72,3584]{1,0:T(8,128)(2,1)S(1)} collective-permute-done((bf16[72,3584]{1,0:T(8,128)(2,1)S(1)}, bf16[72,3584]{1,0:T(8,128)(2,1)S(1)}, u32[]{:S(2)}, u32[]{:S(2)}) %collective-permute-start.5) | collective-permute-done | bytes 516128 | tf_op jit(solution)/shard_map/ppermute | solution.py:23
  116.2 1.6 collective-permute-done.3.above
  117.8 1.3 shard_map.97
  119.1 7.2 %all-to-all-start.1 = ((bf16[4,72,896]{2,1,0:T(8,128)(2,1)}), bf16[4,72,896]{2,1,0:T(8,128)(2,1)S(1)}, u32[]{:S(2)}, u32[]{:S(2)}) async-start(bf16[4,72,896]{2,1,0:T(8,128)(2,1)} %bitcast.10), calls=%async_computation.1 | async-start | bytes 1032192 | tf_op jit(solution)/shard_map/all_to_all | solution.py:222
  127.9 21.6 %all-to-all-done.1 = bf16[4,72,896]{2,1,0:T(8,128)(2,1)S(1)} async-done(((bf16[4,72,896]{2,1,0:T(8,128)(2,1)}), bf16[4,72,896]{2,1,0:T(8,128)(2,1)S(1)}, u32[]{:S(2)}, u32[]{:S(2)}) %all-to-all-start.1) | async-done | bytes 516128 | tf_op jit(solution)/shard_map/all_to_all | solution.py:222
  150.2 2.0 %all_gather.16 = bf16[2,72,1024]{2,1,0:T(8,128)(2,1)S(1)} all-gather(bf16[1,72,1024]{2,1,0:T(8,128)(2,1)S(1)} %pad_maximum_fusion), channel_id=1, replica_groups=mesh['za'=4,'zb'=2,'zd'=2,'x'=4,'y'=8,'c'=2] {'c'}, dimensions={0}, use_global_device_ids=true | all-gather | bytes 442368 | tf_op jit(solution)/shard_map/all_gather | solution.py:27
  152.8 22.9 %all_to_all.15.mine = bf16[32,8,1024]{2,1,0:T(8,128)(2,1)} all-to-all(bf16[32,8,1024]{2,1,0:T(8,128)(2,1)S(1)} %fusion), channel_id=1, replica_groups=mesh['za'=4,'zb'=2,'zd'=2,'x'=4,'y'=8,'c'=2] {'x','y'}, dimensions={0} | all-to-all | bytes 1048576 | tf_op jit(solution)/shard_map/all_to_all | solution.py:240
  175.7 1.7 shard_map.98
  (72 shorter events, 6.6 us)
Async XLA Ops:
  2.2 29.6 %all-to-all-start = ((bf16[32,8,896]{2,1,0:T(8,128)(2,1)}), bf16[32,8,896]{2,1,0:T(8,128)(2,1)S(1)}, u32[]{:S(2)}, u32[]{:S(2)}) async-start(bf16[32,8,896]{2,1,0:T(8,128)(2,1)} %shard_map.94), calls=%async_computation | async-start | bytes 917504 | tf_op jit(solution)/shard_map/all_to_all | solution.py:142
  18.9 13.0 %copy-start.7 = (pred[144]{0:T(512)(128)(4,1)}, pred[144]{0:T(512)(128)(4,1)S(1)}, u32[]{:S(2)}) copy-start(pred[144]{0:T(512)(128)(4,1)S(1)} %get-tuple-element.31) | copy-start | bytes 436
  18.9 12.9 %copy-start.9 = (pred[144]{0:T(512)(128)(4,1)}, pred[144]{0:T(512)(128)(4,1)S(1)}, u32[]{:S(2)}) copy-start(pred[144]{0:T(512)(128)(4,1)S(1)} %get-tuple-element.32) | copy-start | bytes 436
  18.9 12.9 %copy-start.11 = (pred[256]{0:T(512)(128)(4,1)}, pred[256]{0:T(512)(128)(4,1)S(1)}, u32[]{:S(2)}) copy-start(pred[256]{0:T(512)(128)(4,1)S(1)} %compare_and_fusion.1) | copy-start | bytes 772
  18.9 0.7 copy-start.5
  19.6 0.7 copy-start.6
  20.5 11.4 %copy-start.13 = (pred[144]{0:T(512)(128)(4,1)}, pred[144]{0:T(512)(128)(4,1)S(1)}, u32[]{:S(2)}) copy-start(pred[144]{0:T(512)(128)(4,1)S(1)} %iota_compare_fusion.4) | copy-start | bytes 436
  77.9 7.3 %copy-start = (bf16[1,3584,128]{2,1,0:T(8,128)(2,1)S(1)}, bf16[1,3584,128]{2,1,0:T(8,128)(2,1)}, u32[]{:S(2)}) copy-start(bf16[1,3584,128]{2,1,0:T(8,128)(2,1)} %param.10) | copy-start | bytes 2752516
  77.9 7.3 %copy-start.1 = (bf16[1,3584,128]{2,1,0:T(8,128)(2,1)S(1)}, bf16[1,3584,128]{2,1,0:T(8,128)(2,1)}, u32[]{:S(2)}) copy-start(bf16[1,3584,128]{2,1,0:T(8,128)(2,1)} %param.11) | copy-start | bytes 2752516
  78.0 19.7 %collective-permute-start = (bf16[288,896]{1,0:T(8,128)(2,1)S(1)}, bf16[288,896]{1,0:T(8,128)(2,1)}, u32[]{:S(2)}, u32[]{:S(2)}) collective-permute-start(bf16[288,896]{1,0:T(8,128)(2,1)S(1)} %get-tuple-element.18.low), channel_id=1, source_target_pairs={{0,64},{64,128},{128,192},{192,256},{256,320},{320,384},{384,448},... | collective-permute-start | bytes 1548296 | tf_op jit(solution)/shard_map/ppermute | solution.py:23
  81.6 16.1 %collective-permute-start.1 = (bf16[288,896]{1,0:T(8,128)(2,1)S(1)}, bf16[288,896]{1,0:T(8,128)(2,1)}, u32[]{:S(2)}, u32[]{:S(2)}) collective-permute-start(bf16[288,896]{1,0:T(8,128)(2,1)S(1)} %get-tuple-element.17.high), channel_id=1, source_target_pairs={{0,960},{64,0},{128,64},{192,128},{256,192},{320,256},{384,320},{4... | collective-permute-start | bytes 1548296 | tf_op jit(solution)/shard_map/ppermute | solution.py:23
  85.2 1.2 copy-start.2
  89.9 0.7 copy-start.4
  90.6 12.3 %collective-permute-start.4 = (bf16[72,1792]{1,0:T(8,128)(2,1)}, bf16[72,1792]{1,0:T(8,128)(2,1)}, u32[]{:S(2)}, u32[]{:S(2)}) collective-permute-start(bf16[72,1792]{1,0:T(8,128)(2,1)} %get-tuple-element.12), channel_id=1, source_target_pairs={{0,64},{64,128},{128,192},{192,256},{256,320},{320,384},{384,448},... | collective-permute-start | bytes 774152 | tf_op jit(solution)/shard_map/ppermute | solution.py:23
  93.4 12.5 %collective-permute-start.2 = (bf16[72,1792]{1,0:T(8,128)(2,1)}, bf16[72,1792]{1,0:T(8,128)(2,1)S(1)}, u32[]{:S(2)}, u32[]{:S(2)}) collective-permute-start(bf16[72,1792]{1,0:T(8,128)(2,1)} %copy-done.4), channel_id=1, source_target_pairs={{0,960},{64,0},{128,64},{192,128},{256,192},{320,256},{384,320},{4... | collective-permute-start | bytes 774152 | tf_op jit(solution)/shard_map/ppermute | solution.py:23
  97.7 1.2 copy-start.3
  104.0 12.2 %collective-permute-start.5 = (bf16[72,3584]{1,0:T(8,128)(2,1)S(1)}, bf16[72,3584]{1,0:T(8,128)(2,1)S(1)}, u32[]{:S(2)}, u32[]{:S(2)}) collective-permute-start(bf16[72,3584]{1,0:T(8,128)(2,1)S(1)} %fusion.8), channel_id=1, source_target_pairs={{0,64},{64,128},{128,192},{192,256},{256,320},{320,384},{384,448},... | collective-permute-start | bytes 1548296 | tf_op jit(solution)/shard_map/ppermute | solution.py:23
  106.0 11.7 %collective-permute-start.3 = (bf16[72,3584]{1,0:T(8,128)(2,1)S(1)}, bf16[72,3584]{1,0:T(8,128)(2,1)S(1)}, u32[]{:S(2)}, u32[]{:S(2)}) collective-permute-start(bf16[72,3584]{1,0:T(8,128)(2,1)S(1)} %fusion.7), channel_id=1, source_target_pairs={{0,960},{64,0},{128,64},{192,128},{256,192},{320,256},{384,320},{4... | collective-permute-start | bytes 1548296 | tf_op jit(solution)/shard_map/ppermute | solution.py:23
  119.1 30.5 %all-to-all-start.1 = ((bf16[4,72,896]{2,1,0:T(8,128)(2,1)}), bf16[4,72,896]{2,1,0:T(8,128)(2,1)S(1)}, u32[]{:S(2)}, u32[]{:S(2)}) async-start(bf16[4,72,896]{2,1,0:T(8,128)(2,1)} %bitcast.10), calls=%async_computation.1 | async-start | bytes 1032192 | tf_op jit(solution)/shard_map/all_to_all | solution.py:222
  126.3 0.7 copy-start.16
  127.0 0.6 copy-start.8
  127.0 0.7 copy-start.10
  127.0 0.7 copy-start.12
  127.0 0.7 copy-start.14
  (1 other events, 0.6 us)

commit v6 on v4

--- a/solution.py
+++ b/solution.py
@@ -44,7 +44,7 @@
 
 
 def expert_kernel(zb_last, low_hbm, high_hbm, gate_hbm, up_hbm, down_hbm, *refs):
-    outs, (low, high, w_gate, w_up, w_down, sems) = refs[:-6], refs[-6:]
+    outs, (low, high, w_gate, w_up, w_down, stage, sems, out_sems) = refs[:-8], refs[-8:]
     loads = [
         pltpu.make_async_copy(source, target, sems.at[i])
         for i, (source, target) in enumerate(
@@ -105,6 +105,7 @@
     hid_rows = dot(one_hot(taken == jnp.where(second == 0, source, -1)), hid).astype(BF16)
     grad_rows = dot(one_hot(taken == jnp.where(second == 1, source, -1)), grads).astype(BF16)
     first, last = outs[: len(outs) // 2 + len(outs) % 2], outs[-(len(outs) // 2) :]
+    stores = []
     for q in range(QN):
         cols = slice(q * lanes, (q + 1) * lanes)
         pair = jnp.concatenate([w_gate[cols, :], w_up[cols, :]], axis=1)
@@ -112,7 +113,14 @@
         for kind, parts in enumerate((first, last)):
             each = QN // len(parts)
             target = slice(q % each * lanes, (q % each + 1) * lanes)
-            parts[q // each][:, target] = term[kind * group : (kind + 1) * group].astype(BF16)
+            stage[kind, q] = term[kind * group : (kind + 1) * group].astype(BF16)
+            store = pltpu.make_async_copy(
+                stage.at[kind, q], parts[q // each].at[:, target], out_sems.at[kind, q]
+            )
+            store.start()
+            stores.append(store)
+    for store in stores:
+        store.wait()
 
 
 def pack_kernel(source, here, above, below, out):
@@ -206,7 +214,9 @@
             out_shape=[jax.ShapeDtypeStruct((group, w), BF16) for w in width_of],
             in_specs=[pl.BlockSpec(memory_space=pltpu.SMEM)] + [hbm] * 5,
             scratch_shapes=[pltpu.VMEM(v.shape, BF16) for v in (lower, upper) + weights]
-            + [pltpu.SemaphoreType.DMA((5,))],
+            + [pltpu.VMEM((2, QN, group, lanes), BF16)]
+            + [pltpu.SemaphoreType.DMA((5,)), pltpu.SemaphoreType.DMA((2, QN))],
+            out_specs=[hbm for _ in width_of],
             compiler_params=pltpu.CompilerParams(vmem_limit_bytes=62 * 2**20),
             cost_estimate=pl.CostEstimate(
                 flops=36 * group * width * w_down.shape[0],
@@ -219,23 +229,13 @@
 
     back_left = shift_z(far_left, -1)
     back_right = shift_z(far_right, 1)
-    terms_below, terms_above = expert_terms(
-        jnp.where(zd == 1, 1 - zb, zb), from_below, from_above, (1, 1)
+    below_left, below_right, above_left, above_right = expert_terms(
+        jnp.where(zd == 1, 1 - zb, zb), from_below, from_above, (2, 2)
     )
-    low = jnp.concatenate(
-        [
-            (terms_below[:, :half_width].astype(F32) + back_left.astype(F32)).astype(BF16),
-            terms_below[:, half_width:],
-        ],
-        axis=1,
-    )
-    high = jnp.concatenate(
-        [
-            terms_above[:, :half_width],
-            (terms_above[:, half_width:].astype(F32) + back_right.astype(F32)).astype(BF16),
-        ],
-        axis=1,
-    )
+    met_left = (below_left.astype(F32) + back_left.astype(F32)).astype(BF16)
+    met_right = (above_right.astype(F32) + back_right.astype(F32)).astype(BF16)
+    low = jnp.concatenate([met_left, below_right], axis=1)
+    high = jnp.concatenate([above_left, met_right], axis=1)
     row = jnp.arange(ZA * PACK, dtype=jnp.int32)[:, None]
     source = (row // CAP % QN) * group + (row // (QN * CAP) % 2 * ZA + row // PACK) * CAP
     outgoing = pl.pallas_call(

time: 177 us -> 178 us (level)
  transfers between devices with their start and end apart: 8 -> 8, of which waited for: 4 -> 4; matrix products, arithmetic and copies ran while one was open for 1% -> 1% of each run, Pallas kernels for 6% -> 5%
where the time goes in v6:
time: 178 us; the launch traced here: 177 us
  blocking collectives  70.7 us (40%)
  starting transfers between devices  45 us (25%)
  waiting for transfers between devices  40.3 us (23%)
  Pallas kernels  14.1 us (8%)
  local copies, waits for them, and re-layouts  2.42 us (1%)
  other arithmetic  2.3 us (1%)
    all_gather x1, blocking collectives, local(): same = lax.all_gather(packed, ('za', 'zb'), axis=0, tiled=True)  43.7 us
    all_to_all x1, blocking collectives, local(): mine = lax.all_to_all(dense, PLANE, 0, 0, tiled=True)  23 us
    all_to_all x1, waiting for transfers between devices, local(): arrived = lax.all_to_all(outgoing, 'za', 0, 0, tiled=True)  22.7 us
    ppermute x6, starting transfers between devices, shift_z(): return lax.ppermute(values, ZAXES, [(i, (i + step) % n) for i in range(n)])  21.4 us
    all_to_all x1, starting transfers between devices, local(): lax.all_to_all(spread, PLANE, 0, 0, tiled=True)  16.6 us
    all_to_all x1, waiting for transfers between devices, local(): lax.all_to_all(spread, PLANE, 0, 0, tiled=True)  11.2 us
    pallas_call x2, Pallas kernels, expert_terms(): pl.pallas_call(expert_kernel, out_shape=[jax.ShapeDtypeStruct((group, w),...  9.5 us
    all_to_all x1, starting transfers between devices, local(): arrived = lax.all_to_all(outgoing, 'za', 0, 0, tiled=True)  6.95 us
  transfers between devices with their start and end apart: 8, of which 4 were waited for; matrix products, arithmetic and copies ran while one was open for 1% of the time, Pallas kernels for 5%

profile of v6, /device:TPU:8, one launch (start us, length us, event | category | flops | bytes accessed | tf_op | source)
XLA Modules:
  0.0 177.2 jit_solution(16231909689911835712)
XLA Ops:
  0.6 1.6 shard_map.94
  2.2 16.6 %all-to-all-start = ((bf16[32,8,896]{2,1,0:T(8,128)(2,1)}), bf16[32,8,896]{2,1,0:T(8,128)(2,1)S(1)}, u32[]{:S(2)}, u32[]{:S(2)}) async-start(bf16[32,8,896]{2,1,0:T(8,128)(2,1)} %shard_map.94), calls=%async_computation | async-start | bytes 917504 | tf_op jit(solution)/shard_map/all_to_all | solution.py:169
  18.9 0.7 copy-done.6
  20.6 11.2 %all-to-all-done = bf16[32,8,896]{2,1,0:T(8,128)(2,1)S(1)} async-done(((bf16[32,8,896]{2,1,0:T(8,128)(2,1)}), bf16[32,8,896]{2,1,0:T(8,128)(2,1)S(1)}, u32[]{:S(2)}, u32[]{:S(2)}) %all-to-all-start) | async-done | bytes 458784 | tf_op jit(solution)/shard_map/all_to_all | solution.py:169
  32.2 2.0 %all-gather = bf16[144,896]{1,0:T(8,128)(2,1)S(1)} all-gather(bf16[72,896]{1,0:T(8,128)(2,1)S(1)} %slice.66), channel_id=2, replica_groups=mesh['za'=4,'zb'=2,'zd'=2,'x'=4,'y'=8,'c'=2] {'c'}, dimensions={0}, use_global_device_ids=true | all-gather | bytes 387072 | tf_op jit(solution)/shard_map/all_gather | solution.py:27
  34.3 43.7 %all_gather.15 = bf16[576,896]{1,0:T(8,128)(2,1)S(1)} all-gather(bf16[72,896]{1,0:T(8,128)(2,1)S(1)} %fusion.26), channel_id=1, replica_groups=mesh['za'=4,'zb'=2,'zd'=2,'x'=4,'y'=8,'c'=2] {'za','zb'}, dimensions={0}, use_global_device_ids=true | all-gather | bytes 1161216 | tf_op jit(solution)/shard_map/all_gather | solution.py:203
  78.1 3.3 %collective-permute-start = (bf16[288,896]{1,0:T(8,128)(2,1)S(1)}, bf16[288,896]{1,0:T(8,128)(2,1)}, u32[]{:S(2)}, u32[]{:S(2)}) collective-permute-start(bf16[288,896]{1,0:T(8,128)(2,1)S(1)} %get-tuple-element.22.low_hbm), channel_id=1, source_target_pairs={{0,64},{64,128},{128,192},{192,256},{256,320},{320,384},{384,448},... | collective-permute-start | bytes 1548296 | tf_op jit(solution)/shard_map/ppermute | solution.py:23
  81.4 3.7 %collective-permute-start.1 = (bf16[288,896]{1,0:T(8,128)(2,1)S(1)}, bf16[288,896]{1,0:T(8,128)(2,1)}, u32[]{:S(2)}, u32[]{:S(2)}) collective-permute-start(bf16[288,896]{1,0:T(8,128)(2,1)S(1)} %get-tuple-element.21.high_hbm), channel_id=1, source_target_pairs={{0,960},{64,0},{128,64},{192,128},{256,192},{320,256},{384,320},{4... | collective-permute-start | bytes 1548296 | tf_op jit(solution)/shard_map/ppermute | solution.py:23
  85.2 4.7 %shard_map.95 = (bf16[72,1792]{1,0:T(8,128)(2,1)}, bf16[72,1792]{1,0:T(8,128)(2,1)}, bf16[72,3584]{1,0:T(8,128)(2,1)}) custom-call(s32[1]{0:T(128)} %bitcast.4.zb_last, bf16[288,896]{1,0:T(8,128)(2,1)} %copy-done.2, bf16[288,896]{1,0:T(8,128)(2,1)} %copy-done.1, bf16[3584,128]{1,0:T(8,128)(2,1)} %bitcast.33, bf16[3584,128]{1,0:T(8,128)(2,1)} %bitcast.35, ...), custom_call_target="tpu_custom_call" | custom-call | flops 1189085184 | bytes 5505024 | tf_op jit(solution)/shard_map/pallas_call | solution.py:212
  89.9 2.4 %collective-permute-start.4 = (bf16[72,1792]{1,0:T(8,128)(2,1)}, bf16[72,1792]{1,0:T(8,128)(2,1)S(1)}, u32[]{:S(2)}, u32[]{:S(2)}) collective-permute-start(bf16[72,1792]{1,0:T(8,128)(2,1)} %get-tuple-element.16), channel_id=1, source_target_pairs={{0,64},{64,128},{128,192},{192,256},{256,320},{320,384},{384,448},... | collective-permute-start | bytes 774152 | tf_op jit(solution)/shard_map/ppermute | solution.py:23
  92.4 4.6 %collective-permute-start.2 = (bf16[72,1792]{1,0:T(8,128)(2,1)}, bf16[72,1792]{1,0:T(8,128)(2,1)S(1)}, u32[]{:S(2)}, u32[]{:S(2)}) collective-permute-start(bf16[72,1792]{1,0:T(8,128)(2,1)} %get-tuple-element.12), channel_id=1, source_target_pairs={{0,960},{64,0},{128,64},{192,128},{256,192},{320,256},{384,320},{4... | collective-permute-start | bytes 774152 | tf_op jit(solution)/shard_map/ppermute | solution.py:23
  97.0 4.8 %shard_map.96 = (bf16[72,1792]{1,0:T(8,128)(2,1)}, bf16[72,1792]{1,0:T(8,128)(2,1)}, bf16[72,1792]{1,0:T(8,128)(2,1)}, bf16[72,1792]{1,0:T(8,128)(2,1)}) custom-call(s32[1]{0:T(128)} %bitcast.9.zb_last, bf16[288,896]{1,0:T(8,128)(2,1)} %collective-permute-done.low_hbm, bf16[288,896]{1,0:T(8,128)(2,1)} %collective-permute-done.1.high_hbm, ...), custom_call_target="tpu_custom_call" | custom-call | flops 1189085184 | bytes 5505024 | tf_op jit(solution)/shard_map/pallas_call | solution.py:212
  101.8 1.1 add_convert_fusion
  102.9 2.1 %collective-permute-start.5 = (bf16[72,3584]{1,0:T(8,128)(2,1)S(1)}, bf16[72,3584]{1,0:T(8,128)(2,1)S(1)}, u32[]{:S(2)}, u32[]{:S(2)}) collective-permute-start(bf16[72,3584]{1,0:T(8,128)(2,1)S(1)} %pad_maximum_fusion.1), channel_id=1, source_target_pairs={{0,64},{64,128},{128,192},{192,256},{256,320},{320,384},{384,448},... | collective-permute-start | bytes 1548296 | tf_op jit(solution)/shard_map/ppermute | solution.py:23
  105.1 0.9 copy-done.4
  106.0 5.3 %collective-permute-start.3 = (bf16[72,3584]{1,0:T(8,128)(2,1)S(1)}, bf16[72,3584]{1,0:T(8,128)(2,1)S(1)}, u32[]{:S(2)}, u32[]{:S(2)}) collective-permute-start(bf16[72,3584]{1,0:T(8,128)(2,1)S(1)} %pad_maximum_fusion), channel_id=1, source_target_pairs={{0,960},{64,0},{128,64},{192,128},{256,192},{320,256},{384,320},{4... | collective-permute-start | bytes 1548296 | tf_op jit(solution)/shard_map/ppermute | solution.py:23
  111.5 3.8 %collective-permute-done.5.below = bf16[72,3584]{1,0:T(8,128)(2,1)S(1)} collective-permute-done((bf16[72,3584]{1,0:T(8,128)(2,1)S(1)}, bf16[72,3584]{1,0:T(8,128)(2,1)S(1)}, u32[]{:S(2)}, u32[]{:S(2)}) %collective-permute-start.5) | collective-permute-done | bytes 516128 | tf_op jit(solution)/shard_map/ppermute | solution.py:23
  115.3 2.6 %collective-permute-done.3.above = bf16[72,3584]{1,0:T(8,128)(2,1)S(1)} collective-permute-done((bf16[72,3584]{1,0:T(8,128)(2,1)S(1)}, bf16[72,3584]{1,0:T(8,128)(2,1)S(1)}, u32[]{:S(2)}, u32[]{:S(2)}) %collective-permute-start.3) | collective-permute-done | bytes 516128 | tf_op jit(solution)/shard_map/ppermute | solution.py:23
  117.9 1.3 shard_map.97
  119.2 6.9 %all-to-all-start.1 = ((bf16[4,72,896]{2,1,0:T(8,128)(2,1)}), bf16[4,72,896]{2,1,0:T(8,128)(2,1)S(1)}, u32[]{:S(2)}, u32[]{:S(2)}) async-start(bf16[4,72,896]{2,1,0:T(8,128)(2,1)} %bitcast.10), calls=%async_computation.1 | async-start | bytes 1032192 | tf_op jit(solution)/shard_map/all_to_all | solution.py:248
  126.5 22.7 %all-to-all-done.1 = bf16[4,72,896]{2,1,0:T(8,128)(2,1)S(1)} async-done(((bf16[4,72,896]{2,1,0:T(8,128)(2,1)}), bf16[4,72,896]{2,1,0:T(8,128)(2,1)S(1)}, u32[]{:S(2)}, u32[]{:S(2)}) %all-to-all-start.1) | async-done | bytes 516128 | tf_op jit(solution)/shard_map/all_to_all | solution.py:248
  150.0 2.0 %all_gather.16 = bf16[2,72,1024]{2,1,0:T(8,128)(2,1)S(1)} all-gather(bf16[1,72,1024]{2,1,0:T(8,128)(2,1)S(1)} %pad_maximum_fusion.2), channel_id=1, replica_groups=mesh['za'=4,'zb'=2,'zd'=2,'x'=4,'y'=8,'c'=2] {'c'}, dimensions={0}, use_global_device_ids=true | all-gather | bytes 442368 | tf_op jit(solution)/shard_map/all_gather | solution.py:27
  152.5 23.0 %all_to_all.15.mine = bf16[32,8,1024]{2,1,0:T(8,128)(2,1)} all-to-all(bf16[32,8,1024]{2,1,0:T(8,128)(2,1)S(1)} %fusion), channel_id=1, replica_groups=mesh['za'=4,'zb'=2,'zd'=2,'x'=4,'y'=8,'c'=2] {'x','y'}, dimensions={0} | all-to-all | bytes 1048576 | tf_op jit(solution)/shard_map/all_to_all | solution.py:266
  175.4 1.7 shard_map.98
  (56 shorter events, 3.4 us)
Async XLA Ops:
  2.2 29.6 %all-to-all-start = ((bf16[32,8,896]{2,1,0:T(8,128)(2,1)}), bf16[32,8,896]{2,1,0:T(8,128)(2,1)S(1)}, u32[]{:S(2)}, u32[]{:S(2)}) async-start(bf16[32,8,896]{2,1,0:T(8,128)(2,1)} %shard_map.94), calls=%async_computation | async-start | bytes 917504 | tf_op jit(solution)/shard_map/all_to_all | solution.py:169
  18.9 0.7 copy-start.6
  19.6 0.7 copy-start.7
  78.1 7.1 %copy-start.1 = (bf16[288,896]{1,0:T(8,128)(2,1)}, bf16[288,896]{1,0:T(8,128)(2,1)S(1)}, u32[]{:S(2)}) copy-start(bf16[288,896]{1,0:T(8,128)(2,1)S(1)} %get-tuple-element.21.high_hbm) | copy-start | bytes 1548292
  78.1 7.1 %copy-start.2 = (bf16[288,896]{1,0:T(8,128)(2,1)}, bf16[288,896]{1,0:T(8,128)(2,1)S(1)}, u32[]{:S(2)}) copy-start(bf16[288,896]{1,0:T(8,128)(2,1)S(1)} %get-tuple-element.22.low_hbm) | copy-start | bytes 1548292
  78.1 18.9 %collective-permute-start = (bf16[288,896]{1,0:T(8,128)(2,1)S(1)}, bf16[288,896]{1,0:T(8,128)(2,1)}, u32[]{:S(2)}, u32[]{:S(2)}) collective-permute-start(bf16[288,896]{1,0:T(8,128)(2,1)S(1)} %get-tuple-element.22.low_hbm), channel_id=1, source_target_pairs={{0,64},{64,128},{128,192},{192,256},{256,320},{320,384},{384,448},... | collective-permute-start | bytes 1548296 | tf_op jit(solution)/shard_map/ppermute | solution.py:23
  81.4 15.6 %collective-permute-start.1 = (bf16[288,896]{1,0:T(8,128)(2,1)S(1)}, bf16[288,896]{1,0:T(8,128)(2,1)}, u32[]{:S(2)}, u32[]{:S(2)}) collective-permute-start(bf16[288,896]{1,0:T(8,128)(2,1)S(1)} %get-tuple-element.21.high_hbm), channel_id=1, source_target_pairs={{0,960},{64,0},{128,64},{192,128},{256,192},{320,256},{384,320},{4... | collective-permute-start | bytes 1548296 | tf_op jit(solution)/shard_map/ppermute | solution.py:23
  89.9 11.9 %collective-permute-start.4 = (bf16[72,1792]{1,0:T(8,128)(2,1)}, bf16[72,1792]{1,0:T(8,128)(2,1)S(1)}, u32[]{:S(2)}, u32[]{:S(2)}) collective-permute-start(bf16[72,1792]{1,0:T(8,128)(2,1)} %get-tuple-element.16), channel_id=1, source_target_pairs={{0,64},{64,128},{128,192},{192,256},{256,320},{320,384},{384,448},... | collective-permute-start | bytes 774152 | tf_op jit(solution)/shard_map/ppermute | solution.py:23
  92.4 12.6 %collective-permute-start.2 = (bf16[72,1792]{1,0:T(8,128)(2,1)}, bf16[72,1792]{1,0:T(8,128)(2,1)S(1)}, u32[]{:S(2)}, u32[]{:S(2)}) collective-permute-start(bf16[72,1792]{1,0:T(8,128)(2,1)} %get-tuple-element.12), channel_id=1, source_target_pairs={{0,960},{64,0},{128,64},{192,128},{256,192},{320,256},{384,320},{4... | collective-permute-start | bytes 774152 | tf_op jit(solution)/shard_map/ppermute | solution.py:23
  101.8 1.1 copy-start.5
  102.9 2.1 %copy-start.3 = (bf16[72,1792]{1,0:T(8,128)(2,1)S(1)}, bf16[72,1792]{1,0:T(8,128)(2,1)}, u32[]{:S(2)}) copy-start(bf16[72,1792]{1,0:T(8,128)(2,1)} %get-tuple-element.11) | copy-start | bytes 774148
  102.9 12.3 %collective-permute-start.5 = (bf16[72,3584]{1,0:T(8,128)(2,1)S(1)}, bf16[72,3584]{1,0:T(8,128)(2,1)S(1)}, u32[]{:S(2)}, u32[]{:S(2)}) collective-permute-start(bf16[72,3584]{1,0:T(8,128)(2,1)S(1)} %pad_maximum_fusion.1), channel_id=1, source_target_pairs={{0,64},{64,128},{128,192},{192,256},{256,320},{320,384},{384,448},... | collective-permute-start | bytes 1548296 | tf_op jit(solution)/shard_map/ppermute | solution.py:23
  105.0 0.9 copy-start.4
  106.0 11.9 %copy-start = (bf16[72,3584]{1,0:T(8,128)(2,1)S(1)}, bf16[72,3584]{1,0:T(8,128)(2,1)}, u32[]{:S(2)}) copy-start(bf16[72,3584]{1,0:T(8,128)(2,1)} %get-tuple-element.10.here) | copy-start | bytes 1548292
  106.0 11.9 %collective-permute-start.3 = (bf16[72,3584]{1,0:T(8,128)(2,1)S(1)}, bf16[72,3584]{1,0:T(8,128)(2,1)S(1)}, u32[]{:S(2)}, u32[]{:S(2)}) collective-permute-start(bf16[72,3584]{1,0:T(8,128)(2,1)S(1)} %pad_maximum_fusion), channel_id=1, source_target_pairs={{0,960},{64,0},{128,64},{192,128},{256,192},{320,256},{384,320},{4... | collective-permute-start | bytes 1548296 | tf_op jit(solution)/shard_map/ppermute | solution.py:23
  119.2 30.0 %all-to-all-start.1 = ((bf16[4,72,896]{2,1,0:T(8,128)(2,1)}), bf16[4,72,896]{2,1,0:T(8,128)(2,1)S(1)}, u32[]{:S(2)}, u32[]{:S(2)}) async-start(bf16[4,72,896]{2,1,0:T(8,128)(2,1)} %bitcast.10), calls=%async_computation.1 | async-start | bytes 1032192 | tf_op jit(solution)/shard_map/all_to_all | solution.py:248
